TPU v7x, 256 devices: a whole 4x4x8 slice. The times are simulated.
256 devices in a mesh: head: 4 (over y), expert: 32 (over z, x), batch: 2 (over core).
Axes of the slice: x: 4, y: 4, z: 8, core: 2. Of those that a mesh axis runs over, the one named last changes fastest.
Arguments:
- tokens: bfloat16 [512, 4096], P('batch', 'expert'), may hold values from -3 to 3
- attn_gain: bfloat16 [4096], P('expert'), may hold values from 0.099609375 to 1.8984375
- w_query: bfloat16 [4096, 8192], P('expert', 'head'), may hold values from -0.09375 to 0.09375
- q_gain: bfloat16 [128], replicated, may hold values from 0.099609375 to 1.8984375
- cached_keys: bfloat16 [131072, 512], P('expert', 'head'), may hold values from -400 to 400
- prefix_values: bfloat16 [131072, 512], P('expert', 'head'), may hold values from -6 to 6
- output_weight: bfloat16 [8192, 4096], P('head', 'expert'), may hold values from -0.125 to 0.125
- post_gain: bfloat16 [4096], replicated, may hold values from 0.099609375 to 1.8984375
- routes: int32 [512, 8], P('batch'), may hold values from 0 to 63, all different within a row; in each aligned block of 8 rows (0 to 7, 8 to 15, ...) at most 2 rows name the same one
- route_gates: float32 [512, 8], P('batch'), may hold values from 0.1 to 1
- w_gate: bfloat16 [64, 4096, 1536], P(('expert', 'batch'), None, 'head'), may hold values from -0.09375 to 0.09375
- w_up: bfloat16 [64, 4096, 1536], P(('expert', 'batch'), None, 'head'), may hold values from -0.09375 to 0.09375
- w_down: bfloat16 [64, 1536, 4096], P(('expert', 'batch'), 'head'), may hold values from -0.21875 to 0.21875
Outputs:
- layer_out: bfloat16 [512, 4096], P('batch', 'expert')
Inputs may be any that keep to these rules, and one draw needn't show every extreme that they name: `routes`: each row names 8 different experts; in each aligned block of 8 rows no expert is named by more than 2 rows.
All inputs are finite; a program needn't handle non-finite values.
Results may differ from a plain program's by a relative error of at most 0.019.
The roundings to bfloat16 on the way count: a program that leaves them out, or rounds other values in their place, can miss the bound.
Values may be sent and summed in bfloat16 or wider, within the bound.
A program may use at most 192 MiB of HBM per device.

v0:
```python
import jax
import jax.numpy as jnp
from jax import lax
from jax.sharding import PartitionSpec as P

EPSILON = 1e-06
key_block_limit = 512


def combined_all(part, axis, combine):
    gathered = jax.tree.map(lambda a: lax.all_gather(a, axis), part)

    def take(source):
        return jax.tree.map(lambda a: lax.dynamic_index_in_dim(a, source, 0, False), gathered)

    return lax.fori_loop(
        1, lax.axis_size(axis), lambda source, state: combine(state, take(source)), take(0)
    )


def query_norm(projected, q_gain, head_size):
    token_count = projected.shape[0]
    per_head = projected.reshape(token_count, -1, head_size)
    inverse_rms = lax.rsqrt(jnp.mean(per_head * per_head, axis=-1, keepdims=True) + EPSILON)
    normed = (
        per_head * inverse_rms * (q_gain.astype(jnp.float32) / jnp.sqrt(jnp.float32(head_size)))
    )
    return normed.reshape(token_count, -1).astype(jnp.bfloat16)


def prefix_partial(grouped_queries, cached_keys, prefix_values, head_size):
    key_count = cached_keys.shape[0]
    kv_local = cached_keys.shape[1] // head_size
    block_width = min(key_block_limit, key_count)
    blocked_keys = cached_keys.reshape(key_count // block_width, block_width, kv_local, head_size)
    blocked_values = prefix_values.reshape(
        key_count // block_width, block_width, kv_local, head_size
    )
    row_count = grouped_queries.shape[1]
    start_state = (
        jnp.full((kv_local, row_count), -1e30, jnp.float32),
        jnp.zeros((kv_local, row_count), jnp.float32),
        jnp.zeros((kv_local, row_count, head_size), jnp.float32),
    )

    def attend(running, key_values):
        row_peak, row_denominator, weighted_values = running
        key_block, value_block = key_values
        scores = jnp.einsum(
            "jrd,bjd->jrb", grouped_queries, key_block, preferred_element_type=jnp.float32
        )
        new_peak = jnp.maximum(row_peak, jnp.max(scores, axis=-1))
        rescale = jnp.exp(row_peak - new_peak)
        weights = jnp.exp(scores - new_peak[..., None])
        row_denominator = row_denominator * rescale + jnp.sum(weights, axis=-1)
        weighted_values = weighted_values * rescale[..., None] + jnp.einsum(
            "jrb,bjd->jrd",
            weights.astype(jnp.bfloat16),
            value_block,
            preferred_element_type=jnp.float32,
        )
        return ((new_peak, row_denominator, weighted_values), None)

    result, unused = lax.scan(attend, start_state, (blocked_keys, blocked_values))
    return result


def merge_softmax(left_part, right_part):
    left_peak, left_total, left_sum = left_part
    right_peak, right_total, right_sum = right_part
    top_peak = jnp.maximum(left_peak, right_peak)
    left_scale = jnp.exp(left_peak - top_peak)
    right_scale = jnp.exp(right_peak - top_peak)
    return (
        top_peak,
        left_total * left_scale + right_total * right_scale,
        left_sum * left_scale[..., None] + right_sum * right_scale[..., None],
    )


def slot_tables(my_routes, my_gates, expert_count, capacity):
    rows_here, top_count = my_routes.shape
    flat_routes = my_routes.reshape(-1)
    assign_count = flat_routes.shape[0]
    later_index = lax.broadcasted_iota(jnp.int32, (assign_count, assign_count), 0)
    earlier_index = lax.broadcasted_iota(jnp.int32, (assign_count, assign_count), 1)
    matches = (flat_routes[:, None] == flat_routes[None, :]) & (earlier_index < later_index)
    earlier_count = jnp.sum(matches.astype(jnp.int32), axis=1)
    slot_index = flat_routes * capacity + earlier_count
    places = lax.broadcasted_iota(jnp.int32, (expert_count * capacity, assign_count), 0)
    slot_hits = (
        (places == slot_index[None, :])
        .astype(jnp.float32)
        .reshape(expert_count * capacity, rows_here, top_count)
    )
    dispatch_map = jnp.sum(slot_hits, axis=2)
    combine_map = jnp.sum(slot_hits * my_gates[None, :, :], axis=2).T
    return (dispatch_map, combine_map)


def on_device(
    tokens,
    attn_gain,
    w_query,
    q_gain,
    cached_keys,
    prefix_values,
    output_weight,
    post_gain,
    routes,
    route_gates,
    w_gate,
    w_up,
    w_down,
):
    head_size = q_gain.shape[0]
    expert_devices = lax.axis_size("expert")
    token_block, slab_width = tokens.shape
    scaled = (tokens.astype(jnp.float32) * attn_gain.astype(jnp.float32)).astype(jnp.bfloat16)
    partial_value = jnp.dot(scaled, w_query, preferred_element_type=jnp.float32)
    query_matrix = query_norm(lax.psum(partial_value, "expert"), q_gain, head_size)
    kv_local = cached_keys.shape[1] // head_size
    group_width = query_matrix.shape[1] // (kv_local * head_size)
    grouped_queries = (
        query_matrix.reshape(token_block, kv_local, group_width, head_size)
        .transpose(1, 0, 2, 3)
        .reshape(kv_local, token_block * group_width, head_size)
    )
    row_peak, row_denominator, weighted_values = prefix_partial(
        grouped_queries, cached_keys, prefix_values, head_size
    )
    row_peak, row_denominator, weighted_values = combined_all(
        (row_peak, row_denominator, weighted_values), "expert", merge_softmax
    )
    attended_rows = (weighted_values / row_denominator[..., None]).astype(jnp.bfloat16)
    attended_rows = attended_rows.reshape(kv_local, token_block, group_width, head_size)
    output_weights = output_weight.reshape(kv_local, group_width, head_size, slab_width)
    projected = jnp.einsum(
        "jtgd,jgdo->to", attended_rows, output_weights, preferred_element_type=jnp.float32
    )
    after_attn = (tokens.astype(jnp.float32) + lax.psum(projected, "head")).astype(jnp.bfloat16)
    token_rows = lax.all_to_all(after_attn, "expert", split_axis=0, concat_axis=1, tiled=True)
    wide_rows = token_rows.astype(jnp.float32)
    row_mean = jnp.mean(wide_rows * wide_rows, axis=-1, keepdims=True)
    normed = (wide_rows * lax.rsqrt(row_mean + EPSILON) * post_gain.astype(jnp.float32)).astype(
        jnp.bfloat16
    )
    rows_here = token_rows.shape[0]
    start_row = lax.axis_index("expert") * rows_here
    my_routes = lax.dynamic_slice_in_dim(routes, start_row, rows_here, 0)
    my_gates = lax.dynamic_slice_in_dim(route_gates, start_row, rows_here, 0)
    expert_count = expert_devices * lax.axis_size("batch") * w_gate.shape[0]
    capacity = max(2, rows_here * my_routes.shape[1] // expert_count)
    dispatch_map, combine_map = slot_tables(my_routes, my_gates, expert_count, capacity)
    outgoing = jnp.dot(
        dispatch_map.astype(jnp.bfloat16), normed, preferred_element_type=jnp.float32
    ).astype(jnp.bfloat16)
    outgoing = outgoing.reshape(expert_count, capacity, normed.shape[1])
    received = lax.all_to_all(
        outgoing, ("expert", "batch"), split_axis=0, concat_axis=0, tiled=True
    )
    sources, slot_count, model_width = received.shape
    flat_rows = received.reshape(sources * slot_count, model_width)
    gate_part = jnp.dot(flat_rows, w_gate[0], preferred_element_type=jnp.float32)
    up_part = jnp.dot(flat_rows, w_up[0], preferred_element_type=jnp.float32)
    hidden = (jax.nn.silu(gate_part) * up_part).astype(jnp.bfloat16)
    produced = jnp.dot(hidden, w_down[0], preferred_element_type=jnp.float32).reshape(
        sources, slot_count, model_width
    )
    produced = lax.psum(produced, "head")
    returned = lax.all_to_all(
        produced, ("expert", "batch"), split_axis=0, concat_axis=0, tiled=True
    )
    mixture = jnp.dot(
        combine_map,
        returned.reshape(expert_count * capacity, -1),
        precision=lax.Precision.HIGHEST,
        preferred_element_type=jnp.float32,
    )
    finished = (wide_rows + mixture).astype(jnp.bfloat16)
    return lax.all_to_all(finished, "expert", split_axis=1, concat_axis=0, tiled=True)


def solution(mesh):
    placed = (
        P("batch", "expert"),
        P("expert"),
        P("expert", "head"),
        P(),
        P("expert", "head"),
        P("expert", "head"),
        P("head", "expert"),
        P(),
        P("batch", None),
        P("batch", None),
        P(("expert", "batch"), None, "head"),
        P(("expert", "batch"), None, "head"),
        P(("expert", "batch"), "head", None),
    )
    return jax.shard_map(
        on_device, mesh=mesh, in_specs=placed, out_specs=P("batch", "expert"), check_vma=False
    )
```

profile of v0, /device:TPU:2, one launch (start us, length us, event | category | flops | bytes accessed | tf_op | source)
XLA Modules:
  0.0 1152.0 jit_solution(6378087880158758317)
XLA Ops:
  10.5 156.2 %all-reduce.4.cloned.1.call-done = f32[256,2048]{1,0:T(8,128)} async-done(((f32[256,2048]{1,0:T(8,128)}), f32[256,2048]{1,0:T(8,128)}) %all-reduce.4.cloned.1.call-update) | async-done | bytes 2097168 | tf_op jit(solution)/shard_map/psum | solution.py:121
  178.2 125.9 %while.35 = (s32[]{:T(128)}, f32[1,4096]{1,0:T(1,128)S(1)}, f32[1,4096]{1,0:T(1,128)S(1)}, f32[1,4096,128]{2,1,0:T(8,128)}, bf16[8,512,1,128]{3,1,2,0:T(8,128)(2...) while((s32[]{:T(128)}, f32[1,4096]{1,0:T(1,128)S(1)}, ...), condition=%wide.region_5.6_spmd.clone, body=%wide.region_2.5_spmd.clone.sunk | while | flops 1085820928 | bytes 64488580 | solution.py:64
  178.2 5.8 fusion.74
  193.7 5.8 fusion.74
  199.5 4.7 fusion.76
  209.5 5.8 fusion.74
  215.3 4.7 fusion.76
  225.2 5.8 fusion.74
  231.1 4.7 fusion.76
  241.0 5.8 fusion.74
  256.8 5.8 fusion.74
  272.6 5.8 fusion.74
  288.3 5.8 fusion.74
  305.3 49.1 %all-gather.4 = f32[32,1,4096]{2,1,0:T(1,128)S(1)} all-gather(f32[1,1,4096]{2,1,0:T(1,128)S(1)} %bitcast.147), channel_id=3, replica_groups=mesh['head'=4,'expert'=32,'batch'=2] {'expert'}, dimensions={0}, use_global_device_ids=true | all-gather | bytes 540672 | tf_op jit(solution)/shard_map/all_gather | solution.py:11
  354.4 48.0 %all-gather.3 = f32[32,1,4096]{2,1,0:T(1,128)S(1)} all-gather(f32[1,1,4096]{2,1,0:T(1,128)S(1)} %bitcast.139), channel_id=2, replica_groups=mesh['head'=4,'expert'=32,'batch'=2] {'expert'}, dimensions={0}, use_global_device_ids=true | all-gather | bytes 540672 | tf_op jit(solution)/shard_map/all_gather | solution.py:11
  403.3 335.1 %all-gather.7.cloned.1.call-done = f32[32,4096,128]{2,1,0:T(8,128)} async-done(((f32[1,4096,128]{2,1,0:T(8,128)}), f32[32,4096,128]{2,1,0:T(8,128)}) %all-gather.7.cloned.1.call-update) | async-done | bytes 67108880 | tf_op jit(solution)/shard_map/all_gather | solution.py:11
  741.5 142.6 %while.34 = (s32[]{:T(128)}, f32[1,4096]{1,0:T(1,128)S(1)}, f32[1,4096]{1,0:T(1,128)S(1)}, f32[1,4096,128]{2,1,0:T(8,128)}, f32[32,1,4096]{2,1,0:T(1,128)}, /*in...) while((s32[]{:T(128)}, f32[1,4096]{1,0:T(1,128)S(1)}, ...), condition=%wide.region_7.8_spmd, body=%wide.region_6.7_spmd.sunk | while | flops 1597445 | bytes 6455447 | solution.py:16
  887.2 44.8 %all-reduce.6.cloned.1.call-done = f32[256,128]{1,0:T(8,128)} async-done(((f32[256,128]{1,0:T(8,128)}), f32[256,128]{1,0:T(8,128)}) %all-reduce.6.cloned.1.call-update) | async-done | bytes 131088 | tf_op jit(solution)/shard_map/psum | solution.py:141
  933.5 10.1 all-to-all-start
  943.9 8.4 all-to-all-done
  956.5 35.5 %all_to_all.42 = bf16[64,2,4096]{2,1,0:T(2,128)(2,1)} all-to-all(bf16[64,2,4096]{2,1,0:T(2,128)(2,1)} %reshape.168), channel_id=1, replica_groups=mesh['head'=4,'expert'=32,'batch'=2] {'expert','batch'}, dimensions={0} | all-to-all | bytes 2097152 | tf_op jit(solution)/shard_map/all_to_all | solution.py:159
  1000.5 59.6 %all-reduce.8.cloned.1.call-done = f32[64,2,4096]{2,0,1:T(8,128)} async-done(((f32[64,2,4096]{2,0,1:T(8,128)}), f32[64,2,4096]{2,0,1:T(8,128)}) %all-reduce.8.cloned.1.call-update) | async-done | bytes 2097168 | tf_op jit(solution)/shard_map/psum | solution.py:170
  1063.3 61.7 %all_to_all.43 = f32[64,2,4096]{2,1,0:T(2,128)} all-to-all(f32[64,2,4096]{2,1,0:T(2,128)S(1)} %copy.61), channel_id=1, replica_groups=mesh['head'=4,'expert'=32,'batch'=2] {'expert','batch'}, dimensions={0} | all-to-all | bytes 4194304 | tf_op jit(solution)/shard_map/all_to_all | solution.py:171
  1131.3 13.5 %all_to_all.44 = bf16[8,32,128]{2,0,1:T(8,128)(2,1)S(1)} all-to-all(bf16[8,32,128]{2,0,1:T(8,128)(2,1)S(1)} %fusion.34), channel_id=1, replica_groups=mesh['head'=4,'expert'=32,'batch'=2] {'expert'}, dimensions={1} | all-to-all | bytes 131072 | tf_op jit(solution)/shard_map/all_to_all | solution.py:181
  (192 shorter events, 256.2 us)
Async XLA Ops:
  6.5 991.9 %copy-start = (bf16[1,384,4096]{2,1,0:T(8,128)(2,1)S(1)}, bf16[1,384,4096]{2,1,0:T(8,128)(2,1)}, u32[]{:S(2)}) copy-start(bf16[1,384,4096]{2,1,0:T(8,128)(2,1)} %param.29) | copy-start | bytes 9437188
  6.5 160.1 %all-reduce.4.cloned.1.call-start = ((), (), s32[]{:S(2)}) async-start(), calls=%async_computation.4 | async-start | bytes 4194304 | tf_op jit(solution)/shard_map/psum | solution.py:121
  7.3 3.1 copy-start.12
  10.3 728.1 %all-gather.7.cloned.1.call-start = ((), (), s32[]{:S(2)}) async-start(), calls=%async_computation.7 | async-start | bytes 69206016 | tf_op jit(solution)/shard_map/all_gather | solution.py:11
  172.5 1.6 copy-start.2
  184.0 5.8 copy-start.1
  199.5 5.8 copy-start.1
  215.3 5.8 copy-start.1
  231.1 5.8 copy-start.1
  246.8 5.8 copy-start.1
  262.6 5.8 copy-start.1
  278.4 5.8 copy-start.1
  294.2 5.8 copy-start.1
  304.2 627.8 %all-reduce.6.cloned.1.call-start = ((), (), s32[]{:S(2)}) async-start(), calls=%async_computation.5 | async-start | bytes 262144 | tf_op jit(solution)/shard_map/psum | solution.py:141
  354.4 48.0 %copy-start.4 = (f32[32,1,4096]{2,1,0:T(1,128)}, f32[32,1,4096]{2,1,0:T(1,128)S(1)}, u32[]{:S(2)}) copy-start(f32[32,1,4096]{2,1,0:T(1,128)S(1)} %all-gather.4) | copy-start | bytes 1572868
  402.5 0.8 copy-start.5
  884.0 2.0 copy-start.11
  884.0 47.9 %copy-start.6 = (bf16[256,128]{1,0:T(8,128)(2,1)S(1)}, bf16[256,128]{1,0:T(8,128)(2,1)}, u32[]{:S(2)}) copy-start(bf16[256,128]{1,0:T(8,128)(2,1)} %param.17) | copy-start | bytes 196612
  884.0 59.7 %copy-start.9 = (f32[256,8]{0,1:T(8,128)S(1)}, f32[256,8]{0,1:T(8,128)}, u32[]{:S(2)}) copy-start(f32[256,8]{0,1:T(8,128)} %param.26) | copy-start | bytes 24580
  884.0 59.8 %copy-start.7 = (bf16[4096]{0:T(1024)(128)(2,1)S(1)}, bf16[4096]{0:T(1024)(128)(2,1)}, u32[]{:S(2)}) copy-start(bf16[4096]{0:T(1024)(128)(2,1)} %param.24) | copy-start | bytes 24580
  933.5 18.8 %all-to-all-start = ((bf16[32,8,128]{2,1,0:T(8,128)(2,1)}), bf16[32,8,128]{2,1,0:T(8,128)(2,1)S(1)}, u32[]{:S(2)}, u32[]{:S(2)}) async-start(bf16[32,8,128]{2,1,0:T(8,128)(2,1)} %fusion.44), calls=%async_computation | async-start | bytes 131072 | tf_op jit(solution)/shard_map/all_to_all | solution.py:142
  943.6 116.4 %all-reduce.8.cloned.1.call-start = ((), (), s32[]{:S(2)}) async-start(), calls=%async_computation.6 | async-start | bytes 4194304 | tf_op jit(solution)/shard_map/psum | solution.py:170
  994.2 3.1 copy-start.3
  994.2 3.5 copy-start.10
  (1 other events, 0.7 us)
Sparse Core Ops, SparseCore 0:
  10.9 155.7 all-reduce.3
  304.3 434.1 all-gather.6
  887.3 44.6 all-reduce.5
  1000.6 59.3 all-reduce.7
where the time goes:
time: 1160 us; the launch traced here: 1150 us
  waiting for transfers between devices  604 us (52%)
  blocking collectives  208 us (18%)
  other arithmetic  191 us (16%)
  matrix products  93.5 us (8%)
  local copies, waits for them, and re-layouts  31.4 us (3%)
  between operations  13.3 us (1%)
    all_gather x1, waiting for transfers between devices, combined_all(): gathered = jax.tree.map(lambda a: lax.all_gather(a, axis), part)  335 us
    psum x1, waiting for transfers between devices, on_device(): lax.psum(partial_value, 'expert')  156 us
    add x31, other arithmetic, merge_softmax(): left_sum * left_scale[..., None] + right_sum * right_scale[..., None]  118 us
    all_gather x2, blocking collectives, combined_all(): gathered = jax.tree.map(lambda a: lax.all_gather(a, axis), part)  97.2 us
    all_to_all x1, blocking collectives, on_device(): lax.all_to_all(produced, ('expert', 'batch'), split_axis=0, concat_axis=0...  61.7 us
    psum x1, waiting for transfers between devices, on_device(): produced = lax.psum(produced, 'head')  59.6 us
    dot_general x8, matrix products, attend(): jnp.einsum('jrd,bjd->jrb', grouped_queries, key_block, preferred_element_...  46.2 us
    psum x1, waiting for transfers between devices, on_device(): lax.psum(projected, 'head')  44.8 us
  transfers between devices with their start and end apart: 5, of which 5 were waited for; matrix products, arithmetic and copies ran while one was open for 0% of the time, Pallas kernels for 0%

commit v1 on v0

v1 whole, which is shorter than its diff:
```python
import functools

import jax
import jax.numpy as jnp
from jax import lax
from jax.experimental import pallas as pl
from jax.experimental.pallas import tpu as pltpu
from jax.sharding import PartitionSpec as P

EPSILON = 1e-06
MIB = 1024 * 1024
NX, NZ, NH, NB = 4, 8, 4, 2
NE = NX * NZ
HEAD = 128
KEY_CHUNK = 512
MESH = pl.DeviceIdType.MESH
IN_VMEM = pl.BlockSpec(memory_space=pltpu.VMEM)
IN_ANY = pl.BlockSpec(memory_space=pl.ANY)
DMA = pltpu.SemaphoreType.DMA
NEAR_FIRST_Z = (1, 7, 2, 6, 3, 5, 4)
NEAR_FIRST_X = (1, 3, 2)


def remote(src, dst, send_sem, recv_sem, **where):
    return pltpu.make_async_remote_copy(
        src, dst, send_sem, recv_sem, device_id=where, device_id_type=MESH
    )


def here():
    expert = lax.axis_index("expert")
    return expert, expert // NX, lax.rem(expert, NX)


def signal(**where):
    pl.semaphore_signal(
        pltpu.get_barrier_semaphore(), inc=1, device_id=where, device_id_type=MESH
    )


def greet_lines(z, x):
    @pl.loop(1, NZ)
    def _(k):
        signal(expert=lax.rem(z + k, NZ) * NX + x)

    @pl.loop(1, NX)
    def _(k):
        signal(expert=z * NX + lax.rem(x + k, NX))


def greet_experts(expert):
    @pl.loop(1, NE)
    def _(k):
        signal(expert=lax.rem(expert + k, NE))


def gather_blocks(blocks, zs, zr, xs, xr):
    expert, z, x = here()

    def along_z(k, block, target):
        return remote(
            blocks.at[block], blocks.at[block], zs.at[k], zr.at[k], expert=target * NX + x
        )

    def along_x(j, k, column, target):
        block = lax.rem(z + NZ - j, NZ) * NX + column
        return remote(
            blocks.at[block],
            blocks.at[block],
            xs.at[j * NX + k],
            xr.at[j * NX + k],
            expert=z * NX + target,
        )

    for k in NEAR_FIRST_Z:
        along_z(k, expert, lax.rem(z + k, NZ)).start()
    for k in NEAR_FIRST_X:
        along_x(0, k, x, lax.rem(x + k, NX)).start()
    for j in NEAR_FIRST_Z:
        source = lax.rem(z + NZ - j, NZ)
        along_z(j, source * NX + x, source).wait_recv()
        for k in NEAR_FIRST_X:
            along_x(j, k, x, lax.rem(x + k, NX)).start()
    for j in (0,) + NEAR_FIRST_Z:
        for k in NEAR_FIRST_X:
            column = lax.rem(x + NX - k, NX)
            along_x(j, k, column, column).wait_recv()
    for k in NEAR_FIRST_Z:
        along_z(k, expert, lax.rem(z + k, NZ)).wait_send()
    for j in (0,) + NEAR_FIRST_Z:
        for k in NEAR_FIRST_X:
            along_x(j, k, x, lax.rem(x + k, NX)).wait_send()


def project_kernel(
    tokens, gain, w_query, q_gain, queries,
    scaled, weights, partial, arrived,
    ts, tr, ws, wr, ps, pr, zs, zr, xs, xr,
):
    expert, z, x = here()
    greet_lines(z, x)
    pl.semaphore_wait(pltpu.get_barrier_semaphore(), NZ + NX - 2)
    width = w_query.shape[1] // NX

    def columns(owner):
        return pl.ds(pl.multiple_of(owner * width, width), width)

    def weight_copy(k, owner, source):
        return remote(
            w_query.at[:, columns(owner)], weights.at[source], ws.at[k], wr.at[k],
            expert=z * NX + owner,
        )

    def token_copy(k, target, source):
        return remote(
            scaled.at[source], scaled.at[source], ts.at[k], tr.at[k], expert=z * NX + target
        )

    for k in NEAR_FIRST_X:
        weight_copy(k, lax.rem(x + k, NX), x).start()
    scaled[x] = (tokens[...].astype(jnp.float32) * gain[...].astype(jnp.float32)).astype(
        jnp.bfloat16
    )
    for k in NEAR_FIRST_X:
        token_copy(k, lax.rem(x + k, NX), x).start()
    weights[x] = w_query[:, columns(x)]
    for k in NEAR_FIRST_X:
        source = lax.rem(x + NX - k, NX)
        token_copy(k, source, source).wait_recv()
        weight_copy(k, source, source).wait_recv()
    rows = tokens.shape[0]
    left = jnp.concatenate([scaled[i] for i in range(NX)], axis=1)
    right = weights[...].reshape(NX * tokens.shape[1], width)
    product = jnp.dot(left, right, preferred_element_type=jnp.float32)
    partial[...] = product.reshape(NZ, rows // NZ, width)

    def sum_copy(k, target, source):
        return remote(
            partial.at[target], arrived.at[source], ps.at[k], pr.at[k], expert=target * NX + x
        )

    for k in NEAR_FIRST_Z:
        sum_copy(k, lax.rem(z + k, NZ), z).start()
    arrived[z] = partial[z]
    for k in NEAR_FIRST_Z:
        source = lax.rem(z + NZ - k, NZ)
        sum_copy(k, source, source).wait_recv()
    total = arrived[0]
    for i in range(1, NZ):
        total = total + arrived[i]
    factor = q_gain[...].astype(jnp.float32) / jnp.sqrt(jnp.float32(HEAD))
    heads = []
    for h in range(width // HEAD):
        one = total[:, h * HEAD : (h + 1) * HEAD]
        mean = jnp.mean(one * one, axis=-1, keepdims=True)
        heads.append(one * lax.rsqrt(mean + EPSILON) * factor)
    queries[expert] = jnp.concatenate(heads, axis=0).astype(jnp.bfloat16)
    gather_blocks(queries, zs, zr, xs, xr)
    for k in NEAR_FIRST_X:
        weight_copy(k, lax.rem(x + k, NX), x).wait_send()
        token_copy(k, lax.rem(x + k, NX), x).wait_send()
    for k in NEAR_FIRST_Z:
        sum_copy(k, lax.rem(z + k, NZ), z).wait_send()


def attend_block(queries, keys, values, scores):
    rows, count = scores.shape
    top = None
    for start in range(0, count, KEY_CHUNK):
        part = lax.dot_general(
            queries,
            keys[start : start + KEY_CHUNK, :],
            (((1,), (1,)), ((), ())),
            preferred_element_type=jnp.float32,
        )
        scores[:, start : start + KEY_CHUNK] = part
        for i in range(0, KEY_CHUNK, 128):
            piece = part[:, i : i + 128]
            top = piece if top is None else jnp.maximum(top, piece)
    peak = jnp.max(top, axis=1, keepdims=True)
    total = jnp.zeros((rows, 128), jnp.float32)
    weighted = jnp.zeros((rows, HEAD), jnp.float32)
    for start in range(0, count, KEY_CHUNK):
        probs = jnp.exp(scores[:, start : start + KEY_CHUNK] - peak)
        for i in range(0, KEY_CHUNK, 128):
            total = total + probs[:, i : i + 128]
        weighted = weighted + jnp.dot(
            probs.astype(jnp.bfloat16),
            values[start : start + KEY_CHUNK, :],
            preferred_element_type=jnp.float32,
        )
    total = jnp.sum(total, axis=1, keepdims=True)
    return weighted / total, peak + jnp.log(total)


def attend_kernel(
    queries, keys, values, output_weight, tokens, after,
    scores, averages, logs, their_averages, their_logs, attended, partial, arrived,
    os, orr, ls, lr, zs, zr, xs, xr, hs, hr,
):
    expert, z, x = here()
    head = lax.axis_index("head")
    greet_experts(expert)

    @pl.loop(1, NH)
    def _(k):
        signal(head=lax.rem(head + k, NH))

    pl.semaphore_wait(pltpu.get_barrier_semaphore(), NE - 1 + NH - 1)
    block = queries.shape[1]

    def average_copy(target, source):
        return remote(
            averages.at[target], their_averages.at[source], os.at[target], orr.at[source],
            expert=target,
        )

    def log_copy(target, source):
        return remote(
            logs.at[target], their_logs.at[source], ls.at[target], lr.at[source], expert=target
        )

    @pl.loop(0, NE // 2)
    def _(step):
        pair = lax.rem(expert // 2 + step, NE // 2) * 2
        rows = queries[pl.ds(pair, 2)].reshape(2 * block, HEAD)
        average, log_total = attend_block(rows, keys, values, scores)
        averages[pl.ds(pair, 2)] = average.astype(jnp.bfloat16).reshape(2, block, HEAD)
        wide = jnp.broadcast_to(log_total, (2 * block, 128))
        for i in range(2):
            logs[pair + i] = wide[i * block : (i + 1) * block].T[:8]
        for i in range(2):
            @pl.when(pair + i != expert)
            def _():
                average_copy(pair + i, expert).start()
                log_copy(pair + i, expert).start()

    their_averages[expert] = averages[expert]
    their_logs[expert] = logs[expert]

    @pl.loop(1, NE)
    def _(k):
        source = lax.rem(expert + NE - k, NE)
        log_copy(source, source).wait_recv()
        average_copy(source, source).wait_recv()

    each = their_logs[:, 0, :].T
    share = jnp.exp(each - jnp.max(each, axis=1, keepdims=True))
    share = share / jnp.sum(share, axis=1, keepdims=True)
    total = jnp.zeros((block, HEAD), jnp.float32)
    for i in range(NE):
        total = total + share[:, i : i + 1] * their_averages[i].astype(jnp.float32)
    attended[expert] = total.astype(jnp.bfloat16)
    gather_blocks(attended, zs, zr, xs, xr)

    heads_here = block // (tokens.shape[0] // NZ)
    span = block // heads_here
    everything = attended[...].reshape(NZ, NX, heads_here, span, HEAD)
    left = jnp.concatenate(
        [
            everything[:, i, j].reshape(NZ * span, HEAD)
            for i in range(NX)
            for j in range(heads_here)
        ],
        axis=1,
    )
    product = jnp.dot(left, output_weight[...], preferred_element_type=jnp.float32)
    quarter = tokens.shape[0] // NH
    partial[...] = product.reshape(NH, quarter, product.shape[1])

    def sum_copy(k, target, source):
        return remote(
            partial.at[target], arrived.at[source], hs.at[k], hr.at[k], head=target
        )

    for k in (1, 3, 2):
        sum_copy(k, lax.rem(head + k, NH), head).start()
    arrived[head] = partial[head]
    for k in (1, 3, 2):
        source = lax.rem(head + NH - k, NH)
        sum_copy(k, source, source).wait_recv()
    summed = arrived[0]
    for i in range(1, NH):
        summed = summed + arrived[i]
    mine = tokens[pl.ds(pl.multiple_of(head * quarter, quarter), quarter), :]
    after[...] = (mine.astype(jnp.float32) + summed).astype(jnp.bfloat16)

    @pl.loop(1, NE)
    def _(k):
        target = lax.rem(expert + k, NE)
        log_copy(target, expert).wait_send()
        average_copy(target, expert).wait_send()

    for k in (1, 3, 2):
        sum_copy(k, lax.rem(head + k, NH), head).wait_send()


def slot_matrix(routes, gates, experts, group):
    top, count = routes.shape
    names = lax.broadcasted_iota(jnp.int32, (experts, count), 0)
    chosen = jnp.zeros((experts, count), jnp.float32)
    gate = jnp.zeros((experts, count), jnp.float32)
    for k in range(top):
        hit = names == routes[k : k + 1, :]
        chosen = chosen + hit.astype(jnp.float32)
        gate = gate + jnp.where(hit, gates[k : k + 1, :], 0.0)
    earlier = lax.broadcasted_iota(jnp.int32, (count, count), 0)
    later = lax.broadcasted_iota(jnp.int32, (count, count), 1)
    before = ((earlier < later) & (earlier // group == later // group)).astype(jnp.bfloat16)
    rank = jnp.dot(chosen.astype(jnp.bfloat16), before, preferred_element_type=jnp.float32)
    place = chosen * (rank + 1.0)
    slots = 2 * (count // group)
    shape = (experts, slots, count)
    slot = lax.broadcasted_iota(jnp.int32, shape, 1)
    token = lax.broadcasted_iota(jnp.int32, shape, 2)
    wanted = (slot % 2 + 1).astype(jnp.float32)
    hits = (place[:, None, :] == wanted) & (token // group == slot // 2)
    places = hits.astype(jnp.float32)
    return places, places * gate[:, None, :]


def expert_kernel(
    after, routes, gates, post_gain, w_gate, w_up, w_down, out,
    gate_v, up_v, down_v, outgoing, stage, rows_all, normed, product, parts, back, returned,
    wsem, es, er, fs, fr, gs, gr, bs, br, ys, yr,
):
    expert, z, x = here()
    head = lax.axis_index("head")
    core = lax.axis_index("batch")
    load_gate = pltpu.make_async_copy(w_gate, gate_v, wsem.at[0])
    load_up = pltpu.make_async_copy(w_up, up_v, wsem.at[1])
    load_down = pltpu.make_async_copy(w_down, down_v, wsem.at[2])
    load_gate.start()
    load_up.start()
    load_down.start()
    greet_experts(expert)
    others = [(i, j) for j in range(NB) for i in range(NH) if (i, j) != (0, 0)]
    for i, j in others:
        signal(head=lax.rem(head + i, NH), batch=lax.rem(core + j, NB))
    pl.semaphore_wait(pltpu.get_barrier_semaphore(), NE - 1 + len(others))

    count, width = after.shape
    experts = NE * NB
    slots = rows_all.shape[3]
    places, weights = slot_matrix(routes[...], gates[...], experts, 8)
    picked = jnp.dot(
        places.reshape(experts * slots, count).astype(jnp.bfloat16),
        after[...],
        preferred_element_type=jnp.float32,
    ).astype(jnp.bfloat16)
    outgoing[...] = picked.reshape(NE, NB * slots, width)

    def out_copy(target, source):
        return remote(
            outgoing.at[target], stage.at[source], es.at[target], er.at[source], expert=target
        )

    @pl.loop(1, NE)
    def _(k):
        out_copy(lax.rem(expert + k, NE), expert).start()

    stage[expert] = outgoing[expert]
    groups = parts.shape[0]
    per_group = NE // groups
    own_group = expert // per_group

    def target_of(i, j):
        return lax.rem(head + i, NH), lax.rem(core + j, NB)

    def source_of(i, j):
        return lax.rem(head + NH - i, NH), lax.rem(core + NB - j, NB)

    def forward(g, i, j, to_head, to_core, from_head, from_core):
        return remote(
            stage.at[pl.ds(g * per_group, per_group), pl.ds(pl.multiple_of(to_core * slots, slots), slots)],
            rows_all.at[from_head, from_core, pl.ds(g * per_group, per_group)],
            fs.at[g, i * NB + j],
            fr.at[g, i * NB + j],
            head=to_head,
            batch=to_core,
        )

    @pl.loop(0, groups)
    def _(step):
        g = lax.rem(own_group + groups - step, groups)

        @pl.loop(0, per_group)
        def _(k):
            source = g * per_group + k

            @pl.when(source != expert)
            def _():
                out_copy(source, source).wait_recv()

        for i, j in others:
            to_head, to_core = target_of(i, j)
            forward(g, i, j, to_head, to_core, head, core).start()
        rows_all[head, core, pl.ds(g * per_group, per_group)] = stage[
            pl.ds(g * per_group, per_group), pl.ds(pl.multiple_of(core * slots, slots), slots)
        ]

    @pl.loop(0, groups)
    def _(step):
        g = lax.rem(own_group + groups - step, groups)
        for i, j in others:
            from_head, from_core = source_of(i, j)
            forward(g, i, j, from_head, from_core, from_head, from_core).wait_recv()

    held = NH * NB * slots
    square = jnp.zeros((held, width), jnp.float32)
    for e in range(NE):
        wide = rows_all[:, :, e].reshape(held, width).astype(jnp.float32)
        square = square + wide * wide
    mean = jnp.sum(square, axis=1, keepdims=True) * (1.0 / (NE * width))
    scale = lax.rsqrt(mean + EPSILON)
    for e in range(NE):
        wide = rows_all[:, :, e].reshape(held, width).astype(jnp.float32)
        normed[:, e * width : (e + 1) * width] = (
            wide * scale * post_gain[e : e + 1, :].astype(jnp.float32)
        ).astype(jnp.bfloat16)
    load_gate.wait()
    load_up.wait()
    gate_part = jnp.dot(normed[...], gate_v[...], preferred_element_type=jnp.float32)
    up_part = jnp.dot(normed[...], up_v[...], preferred_element_type=jnp.float32)
    hidden = (gate_part / (1.0 + jnp.exp(-gate_part)) * up_part).astype(jnp.bfloat16)
    load_down.wait()
    span = parts.shape[-1]

    def part_copy(g, i, j, to_head, to_core, from_head, from_core):
        return remote(
            product.at[g, to_head, to_core],
            parts.at[g, from_head, from_core],
            gs.at[g, i * NB + j],
            gr.at[g, i * NB + j],
            head=to_head,
            batch=to_core,
        )

    for g in range(groups):
        made = jnp.dot(
            hidden, down_v[:, g * span : (g + 1) * span], preferred_element_type=jnp.float32
        )
        product[g] = made.astype(jnp.bfloat16).reshape(NH, NB, slots, span)
        for i, j in others:
            to_head, to_core = target_of(i, j)
            part_copy(g, i, j, to_head, to_core, head, core).start()
        parts[g, head, core] = product[g, head, core]

    def back_copy(target, source):
        return remote(
            back.at[target], returned.at[source], bs.at[target], br.at[source], expert=target
        )

    for g in range(groups):
        for i, j in others:
            from_head, from_core = source_of(i, j)
            part_copy(g, i, j, from_head, from_core, from_head, from_core).wait_recv()
        total = parts[g, 0].astype(jnp.float32)
        for i in range(1, NH):
            total = total + parts[g, i].astype(jnp.float32)
        total = total.reshape(NB * slots, span).astype(jnp.bfloat16)
        for k in range(per_group):
            back[g * per_group + k] = total[:, k * width : (k + 1) * width]

        @pl.loop(0, per_group)
        def _(k):
            target = g * per_group + k

            @pl.when(target != expert)
            def _():
                back_copy(target, expert).start()

    returned[expert] = back[expert]

    @pl.loop(1, NE)
    def _(k):
        source = lax.rem(expert + NE - k, NE)
        back_copy(source, source).wait_recv()

    flat = weights.reshape(experts * slots, count)
    high = flat.astype(jnp.bfloat16)
    low = (flat - high.astype(jnp.float32)).astype(jnp.bfloat16)
    both = lax.dot_general(
        jnp.concatenate([high, low], axis=1),
        returned[...].reshape(experts * slots, width),
        (((0,), (0,)), ((), ())),
        preferred_element_type=jnp.float32,
    )
    mixture = both[:count] + both[count:]

    def rows_of(owner):
        return pl.ds(pl.multiple_of(owner * count, count), count)

    out[rows_of(head), :] = (after[...].astype(jnp.float32) + mixture).astype(jnp.bfloat16)

    def final_copy(k, target, source):
        return remote(
            out.at[rows_of(source)], out.at[rows_of(source)], ys.at[k], yr.at[k], head=target
        )

    for k in (1, 3, 2):
        final_copy(k, lax.rem(head + k, NH), head).start()
    for k in (1, 3, 2):
        source = lax.rem(head + NH - k, NH)
        final_copy(k, source, source).wait_recv()

    @pl.loop(1, NE)
    def _(k):
        target = lax.rem(expert + k, NE)
        out_copy(target, expert).wait_send()
        back_copy(target, expert).wait_send()

    @pl.loop(0, groups)
    def _(g):
        for i, j in others:
            to_head, to_core = target_of(i, j)
            forward(g, i, j, to_head, to_core, head, core).wait_send()
            part_copy(g, i, j, to_head, to_core, head, core).wait_send()

    for k in (1, 3, 2):
        final_copy(k, lax.rem(head + k, NH), head).wait_send()


def params(collective_id, mib):
    return pltpu.CompilerParams(
        collective_id=collective_id, has_side_effects=True, vmem_limit_bytes=mib * MIB
    )


def on_device(
    tokens, attn_gain, w_query, q_gain, cached_keys, prefix_values, output_weight,
    post_gain, routes, route_gates, w_gate, w_up, w_down,
):
    rows, width = tokens.shape
    block = rows * w_query.shape[1] // HEAD // NE
    bf16, f32 = jnp.bfloat16, jnp.float32
    queries = pl.pallas_call(
        project_kernel,
        out_shape=jax.ShapeDtypeStruct((NE, block, HEAD), bf16),
        in_specs=[IN_VMEM] * 4,
        out_specs=IN_VMEM,
        scratch_shapes=[
            pltpu.VMEM((NX, rows, width), bf16),
            pltpu.VMEM((NX, width, w_query.shape[1] // NX), bf16),
            pltpu.VMEM((NZ, rows // NZ, w_query.shape[1] // NX), f32),
            pltpu.VMEM((NZ, rows // NZ, w_query.shape[1] // NX), f32),
            DMA((NX,)), DMA((NX,)), DMA((NX,)), DMA((NX,)),
            DMA((NZ,)), DMA((NZ,)),
            DMA((NZ,)), DMA((NZ,)), DMA((NZ * NX,)), DMA((NZ * NX,)),
        ],
        compiler_params=params(1, 24),
        name="project_queries",
    )(tokens, attn_gain[None, :], w_query, q_gain[None, :])

    keys = cached_keys.shape[0]
    quarter = rows // NH
    after = pl.pallas_call(
        attend_kernel,
        out_shape=jax.ShapeDtypeStruct((quarter, width), bf16),
        in_specs=[IN_VMEM] * 5,
        out_specs=IN_VMEM,
        scratch_shapes=[
            pltpu.VMEM((2 * block, keys), f32),
            pltpu.VMEM((NE, block, HEAD), bf16),
            pltpu.VMEM((NE, 8, block), f32),
            pltpu.VMEM((NE, block, HEAD), bf16),
            pltpu.VMEM((NE, 8, block), f32),
            pltpu.VMEM((NE, block, HEAD), bf16),
            pltpu.VMEM((NH, quarter, width), f32),
            pltpu.VMEM((NH, quarter, width), f32),
            DMA((NE,)), DMA((NE,)), DMA((NE,)), DMA((NE,)),
            DMA((NZ,)), DMA((NZ,)), DMA((NZ * NX,)), DMA((NZ * NX,)),
            DMA((NH,)), DMA((NH,)),
        ],
        compiler_params=params(2, 40),
        name="attend_prefix",
    )(queries, cached_keys, prefix_values, output_weight, tokens)

    start = lax.axis_index("head") * quarter
    my_routes = lax.dynamic_slice_in_dim(routes, start, quarter, 0).T
    my_gates = lax.dynamic_slice_in_dim(route_gates, start, quarter, 0).T
    model, ff = w_gate.shape[1:]
    slots = 2 * quarter // 8
    groups = 4
    return pl.pallas_call(
        expert_kernel,
        out_shape=jax.ShapeDtypeStruct((rows, width), bf16),
        in_specs=[IN_VMEM] * 4 + [IN_ANY] * 3,
        out_specs=IN_VMEM,
        scratch_shapes=[
            pltpu.VMEM((model, ff), bf16),
            pltpu.VMEM((model, ff), bf16),
            pltpu.VMEM((ff, model), bf16),
            pltpu.VMEM((NE, NB * slots, width), bf16),
            pltpu.VMEM((NE, NB * slots, width), bf16),
            pltpu.VMEM((NH, NB, NE, slots, width), bf16),
            pltpu.VMEM((NH * NB * slots, model), bf16),
            pltpu.VMEM((groups, NH, NB, slots, model // groups), bf16),
            pltpu.VMEM((groups, NH, NB, slots, model // groups), bf16),
            pltpu.VMEM((NE, NB * slots, width), bf16),
            pltpu.VMEM((NE, NB * slots, width), bf16),
            DMA((3,)), DMA((NE,)), DMA((NE,)),
            DMA((groups, NH * NB)), DMA((groups, NH * NB)),
            DMA((groups, NH * NB)), DMA((groups, NH * NB)),
            DMA((NE,)), DMA((NE,)), DMA((NH,)), DMA((NH,)),
        ],
        compiler_params=params(3, 40),
        name="routed_experts",
    )(
        after, my_routes, my_gates, post_gain.reshape(NE, width),
        w_gate[0], w_up[0], w_down[0],
    )


def solution(mesh):
    placed = (
        P("batch", "expert"),
        P("expert"),
        P("expert", "head"),
        P(),
        P("expert", "head"),
        P("expert", "head"),
        P("head", "expert"),
        P(),
        P("batch", None),
        P("batch", None),
        P(("expert", "batch"), None, "head"),
        P(("expert", "batch"), None, "head"),
        P(("expert", "batch"), "head", None),
    )
    return jax.shard_map(
        on_device, mesh=mesh, in_specs=placed, out_specs=P("batch", "expert"), check_vma=False
    )
```

time: 1160 us -> 181 us (0.16)
  waiting for transfers between devices: 604 us -> 0 us
  blocking collectives: 208 us -> 0 us
  other arithmetic: 191 us -> 0 us
  Pallas kernels: 0 us -> 166 us
  matrix products: 93.5 us -> 0 us
  local copies, waits for them, and re-layouts: 31.4 us -> 12.2 us
  between operations: 13.3 us -> 0.06 us
    all_gather x1 -> x0, waiting for transfers between devices: 335 us -> none  [combined_all(): gathered = jax.tree.map(lambda a: lax.all_gather(a, axis), part)]
    psum x3 -> x0, waiting for transfers between devices: 261 us -> none  [the longest x1 156 us: on_device(): lax.psum(partial_value, 'expert')]
    pallas_call x0 -> x3, Pallas kernels: none -> 166 us  [the longest x1 71.9 us: on_device(): pl.pallas_call(attend_kernel, out_shape=jax.ShapeDtypeStruct((quarter, wi...]
    add x71 -> x0, other arithmetic: 143 us -> none  [the longest x31 118 us: merge_softmax(): left_sum * left_scale[..., None] + right_sum * right_scale[..., None]]
    all_to_all x3 -> x0, blocking collectives: 111 us -> none  [the longest x1 61.7 us: on_device(): lax.all_to_all(produced, ('expert', 'batch'), split_axis=0, concat_axis=0...]
    all_gather x2 -> x0, blocking collectives: 97.2 us -> none  [combined_all(): gathered = jax.tree.map(lambda a: lax.all_gather(a, axis), part)]
    dot_general x23 -> x0, matrix products: 93.5 us -> none  [the longest x8 46.2 us: attend(): jnp.einsum('jrd,bjd->jrb', grouped_queries, key_block, preferred_element_...]
    reduce_sum x12 -> x0, other arithmetic: 40.2 us -> none  [the longest x8 37.5 us: attend(): row_denominator = row_denominator * rescale + jnp.sum(weights, axis=-1)]
  transfers between devices with their start and end apart: 5 -> 0, of which waited for: 5 -> 0; matrix products, arithmetic and copies ran while one was open for 0% -> 0% of each run, Pallas kernels for 0% -> 0%
where the time goes in v1:
time: 181 us; the launch traced here: 178 us
  Pallas kernels  166 us (92%)
  local copies, waits for them, and re-layouts  12.2 us (7%)
    pallas_call x1, Pallas kernels, on_device(): pl.pallas_call(attend_kernel, out_shape=jax.ShapeDtypeStruct((quarter, wi...  71.9 us
    pallas_call x1, Pallas kernels, on_device(): pl.pallas_call(expert_kernel, out_shape=jax.ShapeDtypeStruct((rows, width...  47.1 us
    pallas_call x1, Pallas kernels, on_device(): pl.pallas_call(project_kernel, out_shape=jax.ShapeDtypeStruct((NE, block,...  46.5 us
    unnamed x29, local copies, waits for them, and re-layouts  12.1 us

profile of v1, /device:TPU:2, one launch (start us, length us, event | category | flops | bytes accessed | tf_op | source)
XLA Modules:
  0.0 177.8 jit_solution(15698527626156082904)
XLA Ops:
  0.0 0.0 copy-start
  0.0 0.0 copy-start.1
  0.0 0.0 copy-start.7
  0.0 1.2 copy-done.7
  1.2 0.8 copy-done.8
  2.0 0.7 copy-done.11
  2.7 0.7 copy-done.12
  3.3 46.5 %project_queries.1.queries = bf16[32,128,128]{2,1,0:T(8,128)(2,1)S(1)} custom-call(bf16[256,128]{1,0:T(8,128)(2,1)S(1)} %copy-done.8, bf16[1,128]{1,0:T(2,128)(2,1)S(1)} %bitcast.14, bf16[128,2048]{1,0:T(8,128)(2,1)S(1)} %copy-done.7, bf16[1,128]{1,0:T(2,128)(2,1)S(1)} %bitcast.15), custom_call_target="tpu_custom_call" | custom-call | tf_op jit(solution)/shard_map/project_queries/pallas_call | solution.py:537
  49.9 0.0 copy-start.4
  49.9 1.2 copy-done.4
  51.1 1.2 copy-done.5
  52.3 1.0 copy-done.6
  53.4 0.8 copy-done.9
  54.2 71.9 %attend_prefix.1.after = bf16[64,128]{1,0:T(8,128)(2,1)S(1)} custom-call(bf16[32,128,128]{2,1,0:T(8,128)(2,1)S(1)} %project_queries.1.queries, bf16[4096,128]{1,0:T(8,128)(2,1)S(1)} %copy-done.4, bf16[4096,128]{1,0:T(8,128)(2,1)S(1)} %copy-done.5, bf16[2048,128]{1,0:T(8,128)(2,1)S(1)} %copy-done.6, bf16[256,128]{1,0:T(8,128)(2,1)S(1)} %copy-done.9), custom_call_target="tpu_custom_call" | custom-call | tf_op jit(solution)/shard_map/attend_prefix/pallas_call | solution.py:557
  126.1 0.0 copy-done
  126.1 0.1 dynamic-slice_bitcast_fusion.1.routes
  126.2 0.0 copy-done.13
  126.2 0.1 dynamic-slice_bitcast_fusion.gates
  126.3 0.0 copy-done.1
  126.3 0.0 copy-done.10
  126.3 1.9 %copy-done.2 = bf16[1,4096,384]{2,1,0:T(8,128)(2,1)S(1)} copy-done((bf16[1,4096,384]{2,1,0:T(8,128)(2,1)S(1)}, bf16[1,4096,384]{2,1,0:T(8,128)(2,1)}, u32[]{:S(2)}) %copy-start.2) | copy-done | bytes 3145752
  128.2 1.9 %copy-done.3 = bf16[1,384,4096]{2,1,0:T(8,128)(2,1)S(1)} copy-done((bf16[1,384,4096]{2,1,0:T(8,128)(2,1)S(1)}, bf16[1,384,4096]{2,1,0:T(8,128)(2,1)}, u32[]{:S(2)}) %copy-start.3) | copy-done | bytes 3145752
  130.1 47.1 %routed_experts.1 = bf16[256,128]{1,0:T(8,128)(2,1)S(1)} custom-call(bf16[64,128]{1,0:T(8,128)(2,1)S(1)} %attend_prefix.1.after, s32[8,64]{1,0:T(8,128)S(1)} %dynamic-slice_bitcast_fusion.1.routes, f32[8,64]{1,0:T(8,128)S(1)} %dynamic-slice_bitcast_fusion.gates, bf16[32,128]{1,0:T(8,128)(2,1)S(1)} %bitcast.13, bf16[4096,384]{1,0:T(8,128)(2,1)S(1)} %bitcast.10, ...), custom_call_target="tpu_custom_call" | custom-call | tf_op jit(solution)/shard_map/routed_experts/pallas_call | solution.py:585
  177.2 0.6 copy.15
  (10 shorter events, 0.0 us)
Async XLA Ops:
  0.0 126.1 %copy-start = (s32[256,8]{0,1:T(8,128)S(1)}, s32[256,8]{0,1:T(8,128)}, u32[]{:S(2)}) copy-start(s32[256,8]{0,1:T(8,128)} %param.21) | copy-start | bytes 24580
  0.0 126.3 %copy-start.1 = (bf16[1,4096,384]{2,1,0:T(8,128)(2,1)S(1)}, bf16[1,4096,384]{2,1,0:T(8,128)(2,1)}, u32[]{:S(2)}) copy-start(bf16[1,4096,384]{2,1,0:T(8,128)(2,1)} %param.23) | copy-start | bytes 9437188
  0.0 1.2 copy-start.7
  1.2 0.8 copy-start.8
  2.0 0.7 copy-start.11
  2.7 0.7 copy-start.12
  49.9 1.2 copy-start.4
  51.1 1.2 copy-start.5
  52.3 1.0 copy-start.6
  53.4 0.8 copy-start.9
  54.2 72.0 %copy-start.13 = (f32[256,8]{0,1:T(8,128)S(1)}, f32[256,8]{0,1:T(8,128)}, u32[]{:S(2)}) copy-start(f32[256,8]{0,1:T(8,128)} %param.22) | copy-start | bytes 24580
  54.2 72.1 %copy-start.10 = (bf16[4096]{0:T(1024)(128)(2,1)S(1)}, bf16[4096]{0:T(1024)(128)(2,1)}, u32[]{:S(2)}) copy-start(bf16[4096]{0:T(1024)(128)(2,1)} %param.20) | copy-start | bytes 24580
  126.3 1.9 %copy-start.2 = (bf16[1,4096,384]{2,1,0:T(8,128)(2,1)S(1)}, bf16[1,4096,384]{2,1,0:T(8,128)(2,1)}, u32[]{:S(2)}) copy-start(bf16[1,4096,384]{2,1,0:T(8,128)(2,1)} %param.24) | copy-start | bytes 9437188
  128.2 1.9 %copy-start.3 = (bf16[1,384,4096]{2,1,0:T(8,128)(2,1)S(1)}, bf16[1,384,4096]{2,1,0:T(8,128)(2,1)}, u32[]{:S(2)}) copy-start(bf16[1,384,4096]{2,1,0:T(8,128)(2,1)} %param.25) | copy-start | bytes 9437188

commit v2 on v0

v2 whole, which is shorter than its diff:
```python
import functools

import jax
import jax.numpy as jnp
from jax import lax
from jax.experimental import pallas as pl
from jax.experimental.pallas import tpu as pltpu
from jax.sharding import PartitionSpec as P

EPSILON = 1e-06
MIB = 1024 * 1024
NX, NZ, NH, NB = 4, 8, 4, 2
NE = NX * NZ
HEAD = 128
KEY_CHUNK = 256
MESH = pl.DeviceIdType.MESH
IN_VMEM = pl.BlockSpec(memory_space=pltpu.VMEM)
IN_ANY = pl.BlockSpec(memory_space=pl.ANY)
DMA = pltpu.SemaphoreType.DMA
NEAR_FIRST_Z = (1, 7, 2, 6, 3, 5, 4)
NEAR_FIRST_X = (1, 3, 2)


def remote(src, dst, send_sem, recv_sem, **where):
    return pltpu.make_async_remote_copy(
        src, dst, send_sem, recv_sem, device_id=where, device_id_type=MESH
    )


def here():
    expert = lax.axis_index("expert")
    return expert, expert // NX, lax.rem(expert, NX)


def signal(**where):
    pl.semaphore_signal(
        pltpu.get_barrier_semaphore(), inc=1, device_id=where, device_id_type=MESH
    )


def greet_experts(expert):
    @pl.loop(1, NE)
    def _(k):
        signal(expert=lax.rem(expert + k, NE))


def slot_matrix(routes, gates, experts, group):
    top, count = routes.shape
    names = lax.broadcasted_iota(jnp.int32, (experts, count), 0)
    chosen = jnp.zeros((experts, count), jnp.float32)
    gate = jnp.zeros((experts, count), jnp.float32)
    for k in range(top):
        hit = names == routes[k : k + 1, :]
        chosen = chosen + hit.astype(jnp.float32)
        gate = gate + jnp.where(hit, gates[k : k + 1, :], 0.0)
    earlier = lax.broadcasted_iota(jnp.int32, (count, count), 0)
    later = lax.broadcasted_iota(jnp.int32, (count, count), 1)
    before = ((earlier < later) & (earlier // group == later // group)).astype(jnp.bfloat16)
    rank = jnp.dot(chosen.astype(jnp.bfloat16), before, preferred_element_type=jnp.float32)
    place = chosen * (rank + 1.0)
    slots = 2 * (count // group)
    shape = (experts, slots, count)
    slot = lax.broadcasted_iota(jnp.int32, shape, 1)
    token = lax.broadcasted_iota(jnp.int32, shape, 2)
    wanted = (slot % 2 + 1).astype(jnp.float32)
    hits = (place[:, None, :] == wanted) & (token // group == slot // 2)
    places = hits.astype(jnp.float32)
    return places, places * gate[:, None, :]


def transposed_softmax(queries, keys, values_t, scores):
    count, rows = scores.shape
    chunks = range(0, count, KEY_CHUNK)
    top = jnp.full((8, rows), -jnp.inf, jnp.float32)
    for start in chunks:
        part = lax.dot_general(
            keys[start : start + KEY_CHUNK, :],
            queries,
            (((1,), (1,)), ((), ())),
            preferred_element_type=jnp.float32,
        )
        scores[start : start + KEY_CHUNK, :] = part
        top = jnp.maximum(top, jnp.max(part.reshape(KEY_CHUNK // 8, 8, rows), axis=0))
    peak = jnp.max(top, axis=0, keepdims=True)
    total = jnp.zeros((8, rows), jnp.float32)
    weighted = jnp.zeros((HEAD, rows), jnp.float32)
    for start in chunks:
        probs = jnp.exp(scores[start : start + KEY_CHUNK, :] - peak)
        total = total + jnp.sum(probs.reshape(KEY_CHUNK // 8, 8, rows), axis=0)
        weighted = weighted + jnp.dot(
            values_t[:, start : start + KEY_CHUNK],
            probs.astype(jnp.bfloat16),
            preferred_element_type=jnp.float32,
        )
    total = jnp.sum(total, axis=0, keepdims=True)
    return weighted / total, peak + jnp.log(total)


def merged(averages, logs):
    top = logs[0]
    for one in logs[1:]:
        top = jnp.maximum(top, one)
    shares = [jnp.exp(one - top) for one in logs]
    total = shares[0]
    for one in shares[1:]:
        total = total + one
    inverse = 1.0 / total
    result = None
    for one, share in zip(averages, shares):
        term = one.astype(jnp.float32) * (share * inverse)[0:1]
        result = term if result is None else result + term
    return result, top + jnp.log(total)


def layer_kernel(
    tokens, gain, w_query, q_gain, keys_h, values_h, output_h, post_gain, routes, gates,
    w_gate, w_up, w_down, out,
    scaled, weights, partial, arrived, queries, keys, values, values_t, output_weight, scores,
    average_s, log_s, average_x, log_x, merged_s, mlog_s, merged_z, mlog_z, attended,
    part, part_r, after,
    places, mixing, gate_v, up_v, down_v, outgoing, stage, rows_all, normed, product, parts,
    back, returned, final_s, final_r,
    load, ts, tr, ws, wr, ps, pr, qs, qr, fqs, fqr,
    xas, xar, xls, xlr, zas, zar, zls, zlr, ms, mr, fms, fmr, hs, hr,
    es, er, fs, fr, gs, gr, bs, br, ys, yr,
):
    expert, z, x = here()
    head = lax.axis_index("head")
    core = lax.axis_index("batch")
    f32, bf16 = jnp.float32, jnp.bfloat16
    width = w_query.shape[1] // NX
    rows, features = tokens.shape
    block = queries.shape[1]
    span = rows // NZ
    heads_here = width // HEAD
    sub = span // NH
    count = NZ * sub
    others = [(i, j) for j in range(NB) for i in range(NH) if (i, j) != (0, 0)]

    def columns(owner):
        return pl.ds(pl.multiple_of(owner * width, width), width)

    own_weights = pltpu.make_async_copy(w_query.at[:, columns(x)], weights.at[x], load.at[0])
    own_weights.start()
    load_keys = pltpu.make_async_copy(keys_h, keys, load.at[1])
    load_values = pltpu.make_async_copy(values_h, values, load.at[2])
    load_output = pltpu.make_async_copy(output_h, output_weight, load.at[3])
    load_gate = pltpu.make_async_copy(w_gate, gate_v, load.at[4])
    load_up = pltpu.make_async_copy(w_up, up_v, load.at[5])
    load_down = pltpu.make_async_copy(w_down, down_v, load.at[6])

    @pl.loop(1, NE)
    def _(k):
        signal(expert=lax.rem(expert + k, NE))

    for i, j in others:
        signal(head=lax.rem(head + i, NH), batch=lax.rem(core + j, NB))
    scaled[x] = (tokens[...].astype(f32) * gain[...].astype(f32)).astype(bf16)
    pl.semaphore_wait(pltpu.get_barrier_semaphore(), NE - 1 + len(others))

    def weight_copy(k, owner, source):
        return remote(
            w_query.at[:, columns(owner)], weights.at[source], ws.at[k], wr.at[k],
            expert=z * NX + owner,
        )

    def token_copy(k, target, source):
        return remote(
            scaled.at[source], scaled.at[source], ts.at[k], tr.at[k], expert=z * NX + target
        )

    def sum_copy(k, target, source):
        return remote(
            partial.at[target], arrived.at[source], ps.at[k], pr.at[k], expert=target * NX + x
        )

    for k in NEAR_FIRST_X:
        target = lax.rem(x + k, NX)
        token_copy(k, target, x).start()
        weight_copy(k, target, x).start()
    load_keys.start()
    load_values.start()
    load_output.start()
    slots = 2 * count // 8
    experts = NE * NB
    chosen, weighted = slot_matrix(routes[...], gates[...], experts, 8)
    places[...] = chosen.reshape(experts * slots, count).astype(bf16)
    flat = weighted.reshape(experts * slots, count)
    high = flat.astype(bf16)
    mixing[...] = jnp.concatenate([high, (flat - high.astype(f32)).astype(bf16)], axis=1)
    own_weights.wait()
    for k in NEAR_FIRST_X:
        source = lax.rem(x + NX - k, NX)
        token_copy(k, source, source).wait_recv()
        weight_copy(k, source, source).wait_recv()
    left = jnp.concatenate([scaled[i] for i in range(NX)], axis=1)
    right = weights[...].reshape(NX * features, width)
    partial[...] = jnp.dot(left, right, preferred_element_type=f32).reshape(NZ, span, width)
    for k in NEAR_FIRST_Z:
        sum_copy(k, lax.rem(z + k, NZ), z).start()
    arrived[z] = partial[z]
    load_gate.start()
    load_up.start()
    load_down.start()
    load_values.wait()
    for i in range(0, values.shape[0], 128):
        values_t[:, i : i + 128] = values[i : i + 128, :].astype(f32).T.astype(bf16)
    for k in NEAR_FIRST_Z:
        source = lax.rem(z + NZ - k, NZ)
        sum_copy(k, source, source).wait_recv()
    total = arrived[0]
    for i in range(1, NZ):
        total = total + arrived[i]
    factor = q_gain[...].astype(f32) / jnp.sqrt(f32(HEAD))
    heads = []
    for h in range(heads_here):
        one = total[:, h * HEAD : (h + 1) * HEAD]
        mean = jnp.mean(one * one, axis=-1, keepdims=True)
        heads.append(one * lax.rsqrt(mean + EPSILON) * factor)
    queries[expert] = jnp.concatenate(heads, axis=0).astype(bf16)

    def query_z(target, source):
        return remote(
            queries.at[source * NX + x], queries.at[source * NX + x],
            qs.at[target], qr.at[source], expert=target * NX + x,
        )

    def query_x(r, k, target, column):
        return remote(
            queries.at[r * NX + column], queries.at[r * NX + column],
            fqs.at[r * NX + k], fqr.at[r * NX + k], expert=z * NX + target,
        )

    def forward_queries(r):
        @pl.when(r != z)
        def _():
            query_z(r, r).wait_recv()

        for k in NEAR_FIRST_X:
            query_x(r, k, lax.rem(x + k, NX), x).start()

    for k in NEAR_FIRST_Z:
        query_z(lax.rem(z + k, NZ), z).start()
    load_keys.wait()
    load_output.wait()
    ahead = 2
    for r in range(ahead):
        forward_queries(r)

    def average_copy(r, k, target, source):
        return remote(
            average_s.at[r, target], average_x.at[r, source],
            xas.at[r * NX + k], xar.at[r * NX + k], expert=z * NX + target,
        )

    def log_copy(r, k, target, source):
        return remote(
            log_s.at[r, target], log_x.at[r, source],
            xls.at[r * NX + k], xlr.at[r * NX + k], expert=z * NX + target,
        )

    def merged_copy(target, source):
        return remote(
            merged_s.at[target], merged_z.at[source], zas.at[target], zar.at[source],
            expert=target * NX + x,
        )

    def mlog_copy(target, source):
        return remote(
            mlog_s.at[target], mlog_z.at[source], zls.at[target], zlr.at[source],
            expert=target * NX + x,
        )

    def attended_z(target, source):
        return remote(
            attended.at[source * NX + x], attended.at[source * NX + x],
            ms.at[target], mr.at[source], expert=target * NX + x,
        )

    def attended_x(r, k, target, column):
        return remote(
            attended.at[r * NX + column], attended.at[r * NX + column],
            fms.at[r * NX + k], fmr.at[r * NX + k], expert=z * NX + target,
        )

    def head_copy(r, k, target, source):
        return remote(
            part.at[r, target], part_r.at[source, r],
            hs.at[r * NH + k], hr.at[r * NH + k], head=target,
        )

    def attend(r):
        for k in NEAR_FIRST_X:
            column = lax.rem(x + NX - k, NX)
            query_x(r, k, column, column).wait_recv()
        here_rows = queries[pl.ds(r * NX, NX)].reshape(NX * block, HEAD)
        average, log_total = transposed_softmax(here_rows, keys, values_t, scores)
        average = average.astype(bf16)
        log_total = jnp.broadcast_to(log_total, (8, NX * block))
        for i in range(NX):
            average_s[r, i] = average[:, i * block : (i + 1) * block]
            log_s[r, i] = log_total[:, i * block : (i + 1) * block]
        for k in NEAR_FIRST_X:
            target = lax.rem(x + k, NX)
            log_copy(r, k, target, x).start()
            average_copy(r, k, target, x).start()
        average_x[r, x] = average_s[r, x]
        log_x[r, x] = log_s[r, x]

    def merge_x(r):
        for k in NEAR_FIRST_X:
            source = lax.rem(x + NX - k, NX)
            log_copy(r, k, source, source).wait_recv()
            average_copy(r, k, source, source).wait_recv()
        average, log_total = merged(
            [average_x[r, i] for i in range(NX)], [log_x[r, i] for i in range(NX)]
        )
        average = average.astype(bf16)

        @pl.when(r == z)
        def _():
            merged_z[z] = average
            mlog_z[z] = log_total

        @pl.when(r != z)
        def _():
            merged_s[r] = average
            mlog_s[r] = log_total
            mlog_copy(r, z).start()
            merged_copy(r, z).start()

    def merge_z(r):
        @pl.when(r == z)
        def _():
            @pl.loop(1, NZ)
            def _(k):
                source = lax.rem(z + k, NZ)
                mlog_copy(source, source).wait_recv()
                merged_copy(source, source).wait_recv()

            average, _ = merged(
                [merged_z[i] for i in range(NZ)], [mlog_z[i] for i in range(NZ)]
            )
            attended[expert] = average.T.astype(bf16)
            for k in NEAR_FIRST_Z:
                attended_z(lax.rem(z + k, NZ), z).start()

    def forward_attended(r):
        @pl.when(r != z)
        def _():
            attended_z(r, r).wait_recv()

        for k in NEAR_FIRST_X:
            attended_x(r, k, lax.rem(x + k, NX), x).start()

    def project(r):
        for k in NEAR_FIRST_X:
            column = lax.rem(x + NX - k, NX)
            attended_x(r, k, column, column).wait_recv()
        left = jnp.concatenate(
            [
                attended[r * NX + i, j * span : (j + 1) * span, :]
                for i in range(NX)
                for j in range(heads_here)
            ],
            axis=1,
        )
        made = jnp.dot(left, output_weight[...], preferred_element_type=f32)
        part[r] = made.reshape(NH, sub, features)
        for k in (1, 3, 2):
            head_copy(r, k, lax.rem(head + k, NH), head).start()
        part_r[head, r] = part[r, head]

    @pl.loop(0, NZ + 4)
    def _(step):
        @pl.when(step + ahead < NZ)
        def _():
            forward_queries(step + ahead)

        @pl.when(step < NZ)
        def _():
            attend(step)

        for offset, stage_of in ((4, project), (3, forward_attended), (2, merge_z), (1, merge_x)):
            @pl.when((step >= offset) & (step < NZ + offset))
            def _():
                stage_of(step - offset)

    for r in range(NZ):
        for k in (1, 3, 2):
            source = lax.rem(head + NH - k, NH)
            head_copy(r, k, source, source).wait_recv()
    for r in range(NZ):
        summed = part_r[0, r]
        for i in range(1, NH):
            summed = summed + part_r[i, r]
        after[r * sub : (r + 1) * sub, :] = summed
    resid = tokens[...].astype(f32).reshape(NZ, NH, sub, features)
    mine = jnp.zeros((NZ, sub, features), f32)
    for i in range(NH):
        mine = jnp.where(head == i, resid[:, i], mine)
    stream = (mine.reshape(count, features) + after[...]).astype(bf16)

    def out_copy(target, source):
        return remote(
            outgoing.at[target], stage.at[source], es.at[target], er.at[source], expert=target
        )

    picked = jnp.dot(places[...], stream, preferred_element_type=f32).astype(bf16)
    outgoing[...] = picked.reshape(NE, NB * slots, features)

    @pl.loop(1, NE)
    def _(k):
        out_copy(lax.rem(expert + k, NE), expert).start()

    stage[expert] = outgoing[expert]
    groups = parts.shape[0]
    per_group = NE // groups
    own_group = expert // per_group

    def target_of(i, j):
        return lax.rem(head + i, NH), lax.rem(core + j, NB)

    def source_of(i, j):
        return lax.rem(head + NH - i, NH), lax.rem(core + NB - j, NB)

    def half(owner):
        return pl.ds(pl.multiple_of(owner * slots, slots), slots)

    def forward(g, i, j, to_head, to_core, from_head, from_core):
        return remote(
            stage.at[pl.ds(g * per_group, per_group), half(to_core)],
            rows_all.at[from_head, from_core, pl.ds(g * per_group, per_group)],
            fs.at[g, i * NB + j],
            fr.at[g, i * NB + j],
            head=to_head,
            batch=to_core,
        )

    @pl.loop(0, groups)
    def _(step):
        g = lax.rem(own_group + groups - step, groups)

        @pl.loop(0, per_group)
        def _(k):
            source = g * per_group + k

            @pl.when(source != expert)
            def _():
                out_copy(source, source).wait_recv()

        for i, j in others:
            to_head, to_core = target_of(i, j)
            forward(g, i, j, to_head, to_core, head, core).start()
        rows_all[head, core, pl.ds(g * per_group, per_group)] = stage[
            pl.ds(g * per_group, per_group), half(core)
        ]

    load_gate.wait()
    load_up.wait()
    load_down.wait()

    @pl.loop(0, groups)
    def _(step):
        g = lax.rem(own_group + groups - step, groups)
        for i, j in others:
            from_head, from_core = source_of(i, j)
            forward(g, i, j, from_head, from_core, from_head, from_core).wait_recv()

    held = NH * NB * slots
    square = jnp.zeros((held, features), f32)
    for e in range(NE):
        wide = rows_all[:, :, e].reshape(held, features).astype(f32)
        square = square + wide * wide
    mean = jnp.sum(square, axis=1, keepdims=True) * (1.0 / (NE * features))
    scale = lax.rsqrt(mean + EPSILON)
    for e in range(NE):
        wide = rows_all[:, :, e].reshape(held, features).astype(f32)
        normed[:, e * features : (e + 1) * features] = (
            wide * scale * post_gain[e : e + 1, :].astype(f32)
        ).astype(bf16)
    gate_part = jnp.dot(normed[...], gate_v[...], preferred_element_type=f32)
    up_part = jnp.dot(normed[...], up_v[...], preferred_element_type=f32)
    hidden = (gate_part / (1.0 + jnp.exp(-gate_part)) * up_part).astype(bf16)
    reach = parts.shape[-1]

    def part_copy(g, i, j, to_head, to_core, from_head, from_core):
        return remote(
            product.at[g, to_head, to_core],
            parts.at[g, from_head, from_core],
            gs.at[g, i * NB + j],
            gr.at[g, i * NB + j],
            head=to_head,
            batch=to_core,
        )

    for g in range(groups):
        made = jnp.dot(hidden, down_v[:, g * reach : (g + 1) * reach], preferred_element_type=f32)
        product[g] = made.astype(bf16).reshape(NH, NB, slots, reach)
        for i, j in others:
            to_head, to_core = target_of(i, j)
            part_copy(g, i, j, to_head, to_core, head, core).start()
        parts[g, head, core] = product[g, head, core]

    def back_copy(target, source):
        return remote(
            back.at[target], returned.at[source], bs.at[target], br.at[source], expert=target
        )

    for g in range(groups):
        for i, j in others:
            from_head, from_core = source_of(i, j)
            part_copy(g, i, j, from_head, from_core, from_head, from_core).wait_recv()
        total = parts[g, 0].astype(f32)
        for i in range(1, NH):
            total = total + parts[g, i].astype(f32)
        total = total.reshape(NB * slots, reach).astype(bf16)
        for k in range(per_group):
            back[g * per_group + k] = total[:, k * features : (k + 1) * features]

        @pl.loop(0, per_group)
        def _(k):
            target = g * per_group + k

            @pl.when(target != expert)
            def _():
                back_copy(target, expert).start()

    returned[expert] = back[expert]

    @pl.loop(1, NE)
    def _(k):
        source = lax.rem(expert + NE - k, NE)
        back_copy(source, source).wait_recv()

    both = lax.dot_general(
        mixing[...],
        returned[...].reshape(experts * slots, features),
        (((0,), (0,)), ((), ())),
        preferred_element_type=f32,
    )
    mixture = both[:count] + both[count:]
    final_s[...] = (stream.astype(f32) + mixture).astype(bf16)

    def final_copy(k, target, source):
        return remote(final_s, final_r.at[source], ys.at[k], yr.at[k], head=target)

    for k in (1, 3, 2):
        final_copy(k, lax.rem(head + k, NH), head).start()
    final_r[head] = final_s[...]
    for k in (1, 3, 2):
        source = lax.rem(head + NH - k, NH)
        final_copy(k, source, source).wait_recv()
    pieces = [final_r[i].astype(f32).reshape(NZ, sub, features) for i in range(NH)]
    out[...] = jnp.concatenate(
        [pieces[i][r] for r in range(NZ) for i in range(NH)], axis=0
    ).astype(bf16)

    for k in NEAR_FIRST_X:
        target = lax.rem(x + k, NX)
        token_copy(k, target, x).wait_send()
        weight_copy(k, target, x).wait_send()

        @pl.loop(0, NZ)
        def _(r):
            query_x(r, k, target, x).wait_send()
            average_copy(r, k, target, x).wait_send()
            log_copy(r, k, target, x).wait_send()
            attended_x(r, k, target, x).wait_send()

    @pl.loop(1, NZ)
    def _(k):
        target = lax.rem(z + k, NZ)
        sum_copy(k, target, z).wait_send()
        query_z(target, z).wait_send()
        merged_copy(target, z).wait_send()
        mlog_copy(target, z).wait_send()
        attended_z(target, z).wait_send()

    for k in (1, 3, 2):
        target = lax.rem(head + k, NH)
        final_copy(k, target, head).wait_send()

        @pl.loop(0, NZ)
        def _(r):
            head_copy(r, k, target, head).wait_send()

    @pl.loop(1, NE)
    def _(k):
        target = lax.rem(expert + k, NE)
        out_copy(target, expert).wait_send()
        back_copy(target, expert).wait_send()

    @pl.loop(0, groups)
    def _(g):
        for i, j in others:
            to_head, to_core = target_of(i, j)
            forward(g, i, j, to_head, to_core, head, core).wait_send()
            part_copy(g, i, j, to_head, to_core, head, core).wait_send()


def on_device(
    tokens, attn_gain, w_query, q_gain, cached_keys, prefix_values, output_weight,
    post_gain, routes, route_gates, w_gate, w_up, w_down,
):
    rows, features = tokens.shape
    width = w_query.shape[1] // NX
    block = rows * w_query.shape[1] // HEAD // NE
    bf16, f32 = jnp.bfloat16, jnp.float32
    keys = cached_keys.shape[0]
    span = rows // NZ
    sub = span // NH
    count = NZ * sub
    head = lax.axis_index("head")
    top = routes.shape[1]

    def mine(table):
        cut = lax.dynamic_index_in_dim(table.reshape(NZ, NH, sub, top), head, 1, False)
        return cut.reshape(count, top).T

    model, ff = w_gate.shape[1:]
    slots = 2 * count // 8
    groups = 4
    experts = NE * NB
    V = pltpu.VMEM
    return pl.pallas_call(
        layer_kernel,
        out_shape=jax.ShapeDtypeStruct((rows, features), bf16),
        in_specs=[IN_VMEM, IN_VMEM, IN_ANY, IN_VMEM] + [IN_ANY] * 3 + [IN_VMEM] * 3 + [IN_ANY] * 3,
        out_specs=IN_VMEM,
        scratch_shapes=[
            V((NX, rows, features), bf16),
            V((NX, features, width), bf16),
            V((NZ, span, width), f32),
            V((NZ, span, width), f32),
            V((NE, block, HEAD), bf16),
            V((keys, HEAD), bf16),
            V((keys, HEAD), bf16),
            V((HEAD, keys), bf16),
            V(output_weight.shape, bf16),
            V((keys, NX * block), f32),
            V((NZ, NX, HEAD, block), bf16),
            V((NZ, NX, 8, block), f32),
            V((NZ, NX, HEAD, block), bf16),
            V((NZ, NX, 8, block), f32),
            V((NZ, HEAD, block), bf16),
            V((NZ, 8, block), f32),
            V((NZ, HEAD, block), bf16),
            V((NZ, 8, block), f32),
            V((NE, block, HEAD), bf16),
            V((NZ, NH, sub, features), f32),
            V((NH, NZ, sub, features), f32),
            V((count, features), f32),
            V((experts * slots, count), bf16),
            V((experts * slots, 2 * count), bf16),
            V((model, ff), bf16),
            V((model, ff), bf16),
            V((ff, model), bf16),
            V((NE, NB * slots, features), bf16),
            V((NE, NB * slots, features), bf16),
            V((NH, NB, NE, slots, features), bf16),
            V((NH * NB * slots, model), bf16),
            V((groups, NH, NB, slots, model // groups), bf16),
            V((groups, NH, NB, slots, model // groups), bf16),
            V((NE, NB * slots, features), bf16),
            V((NE, NB * slots, features), bf16),
            V((count, features), bf16),
            V((NH, count, features), bf16),
            DMA((7,)),
            DMA((NX,)), DMA((NX,)), DMA((NX,)), DMA((NX,)),
            DMA((NZ,)), DMA((NZ,)),
            DMA((NZ,)), DMA((NZ,)), DMA((NE,)), DMA((NE,)),
            DMA((NE,)), DMA((NE,)), DMA((NE,)), DMA((NE,)),
            DMA((NZ,)), DMA((NZ,)), DMA((NZ,)), DMA((NZ,)),
            DMA((NZ,)), DMA((NZ,)), DMA((NE,)), DMA((NE,)),
            DMA((NZ * NH,)), DMA((NZ * NH,)),
            DMA((NE,)), DMA((NE,)),
            DMA((groups, NH * NB)), DMA((groups, NH * NB)),
            DMA((groups, NH * NB)), DMA((groups, NH * NB)),
            DMA((NE,)), DMA((NE,)), DMA((NH,)), DMA((NH,)),
        ],
        compiler_params=pltpu.CompilerParams(
            collective_id=1, has_side_effects=True, vmem_limit_bytes=56 * MIB
        ),
        name="scoring_layer",
    )(
        tokens, attn_gain[None, :], w_query, q_gain[None, :],
        cached_keys, prefix_values, output_weight,
        post_gain.reshape(NE, features), mine(routes), mine(route_gates),
        w_gate[0], w_up[0], w_down[0],
    )


def solution(mesh):
    placed = (
        P("batch", "expert"),
        P("expert"),
        P("expert", "head"),
        P(),
        P("expert", "head"),
        P("expert", "head"),
        P("head", "expert"),
        P(),
        P("batch", None),
        P("batch", None),
        P(("expert", "batch"), None, "head"),
        P(("expert", "batch"), None, "head"),
        P(("expert", "batch"), "head", None),
    )
    return jax.shard_map(
        on_device, mesh=mesh, in_specs=placed, out_specs=P("batch", "expert"), check_vma=False
    )
```

time: 1160 us -> 161 us (0.14)
  the two profiles are of different devices: /device:TPU:2 before, /device:TPU:224 now
where the time goes in v2:
time: 161 us
  Pallas kernels  156 us (97%)
  local copies, waits for them, and re-layouts  4.66 us (3%)
    pallas_call x1, Pallas kernels, on_device(): pl.pallas_call(layer_kernel, out_shape=jax.ShapeDtypeStruct((rows, featur...  156 us

profile of v2, /device:TPU:224, one launch (start us, length us, event | category | flops | bytes accessed | tf_op | source)
XLA Modules:
  0.0 160.7 jit_solution(1113333021861159938)
XLA Ops:
  0.0 0.9 reshape.18
  0.9 0.7 reshape.19
  1.6 0.9 reshape.20
  2.6 0.7 reshape.21
  3.2 156.0 %scoring_layer.1 = bf16[256,128]{1,0:T(8,128)(2,1)} custom-call(bf16[256,128]{1,0:T(8,128)(2,1)} %tokens.1, bf16[1,128]{1,0:T(2,128)(2,1)} %bitcast.30, bf16[128,2048]{1,0:T(8,128)(2,1)} %w_query.1, bf16[1,128]{1,0:T(2,128)(2,1)} %bitcast.31, bf16[4096,128]{1,0:T(8,128)(2,1)} %keys_h.1, bf16[4096,128]{1,0:T(8,128)(2,1)} %values_h.1, ...), custom_call_target="tpu_custom_call" | custom-call | tf_op jit(solution)/shard_map/scoring_layer/pallas_call | solution.py:626
  159.3 1.5 copy.19
  (2 shorter events, 0.1 us)

commit v3 on v2

v3 whole, which is shorter than its diff:
```python
import functools

import jax
import jax.numpy as jnp
from jax import lax
from jax.experimental import pallas as pl
from jax.experimental.pallas import tpu as pltpu
from jax.sharding import PartitionSpec as P

EPSILON = 1e-06
MIB = 1024 * 1024
NX, NZ, NH, NB = 4, 8, 4, 2
NE = NX * NZ
HEAD = 128
KEY_CHUNK = 256
LOG_ROWS = 16
MESH = pl.DeviceIdType.MESH
IN_VMEM = pl.BlockSpec(memory_space=pltpu.VMEM)
IN_ANY = pl.BlockSpec(memory_space=pl.ANY)
DMA = pltpu.SemaphoreType.DMA
NEAR_FIRST_Z = (1, 7, 2, 6, 3, 5, 4)
NEAR_FIRST_X = (1, 3, 2)


def remote(src, dst, send_sem, recv_sem, **where):
    return pltpu.make_async_remote_copy(
        src, dst, send_sem, recv_sem, device_id=where, device_id_type=MESH
    )


def here():
    expert = lax.axis_index("expert")
    return expert, expert // NX, lax.rem(expert, NX)


def signal(**where):
    pl.semaphore_signal(
        pltpu.get_barrier_semaphore(), inc=1, device_id=where, device_id_type=MESH
    )


def greet_experts(expert):
    @pl.loop(1, NE)
    def _(k):
        signal(expert=lax.rem(expert + k, NE))


def slot_matrix(routes, gates, experts, group):
    top, count = routes.shape
    names = lax.broadcasted_iota(jnp.int32, (experts, count), 0)
    chosen = jnp.zeros((experts, count), jnp.float32)
    gate = jnp.zeros((experts, count), jnp.float32)
    for k in range(top):
        hit = names == routes[k : k + 1, :]
        chosen = chosen + hit.astype(jnp.float32)
        gate = gate + jnp.where(hit, gates[k : k + 1, :], 0.0)
    earlier = lax.broadcasted_iota(jnp.int32, (count, count), 0)
    later = lax.broadcasted_iota(jnp.int32, (count, count), 1)
    before = ((earlier < later) & (earlier // group == later // group)).astype(jnp.bfloat16)
    rank = jnp.dot(chosen.astype(jnp.bfloat16), before, preferred_element_type=jnp.float32)
    place = chosen * (rank + 1.0)
    slots = 2 * (count // group)
    shape = (experts, slots, count)
    slot = lax.broadcasted_iota(jnp.int32, shape, 1)
    token = lax.broadcasted_iota(jnp.int32, shape, 2)
    wanted = (slot % 2 + 1).astype(jnp.float32)
    hits = (place[:, None, :] == wanted) & (token // group == slot // 2)
    places = hits.astype(jnp.float32)
    return places, places * gate[:, None, :]


def transposed_softmax(queries, keys, values_t, scores):
    count, rows = scores.shape
    chunks = range(0, count, KEY_CHUNK)
    top = jnp.full((8, rows), -jnp.inf, jnp.float32)
    for start in chunks:
        part = lax.dot_general(
            keys[start : start + KEY_CHUNK, :],
            queries,
            (((1,), (1,)), ((), ())),
            preferred_element_type=jnp.float32,
        )
        scores[start : start + KEY_CHUNK, :] = part
        top = jnp.maximum(top, jnp.max(part.reshape(KEY_CHUNK // 8, 8, rows), axis=0))
    peak = jnp.max(top, axis=0, keepdims=True)
    total = jnp.zeros((8, rows), jnp.float32)
    weighted = jnp.zeros((HEAD, rows), jnp.float32)
    for start in chunks:
        probs = jnp.exp(scores[start : start + KEY_CHUNK, :] - peak)
        total = total + jnp.sum(probs.reshape(KEY_CHUNK // 8, 8, rows), axis=0)
        weighted = weighted + jnp.dot(
            values_t[:, start : start + KEY_CHUNK],
            probs.astype(jnp.bfloat16),
            preferred_element_type=jnp.float32,
        )
    total = jnp.sum(total, axis=0, keepdims=True)
    return weighted / total, peak + jnp.log(total)


def with_log(average, log_total):
    rows = average.shape[1]
    high = log_total.astype(jnp.bfloat16).astype(jnp.float32)
    rest = log_total - high
    middle = rest.astype(jnp.bfloat16).astype(jnp.float32)
    low = rest - middle
    place = lax.broadcasted_iota(jnp.int32, (LOG_ROWS, rows), 0)
    tail = jnp.where(place == 0, high, jnp.where(place == 1, middle, low))
    return jnp.concatenate([average, tail], axis=0).astype(jnp.bfloat16)


def merged(blocks):
    logs = []
    for block in blocks:
        tail = block[HEAD : HEAD + LOG_ROWS].astype(jnp.float32)
        logs.append(tail[0:1] + tail[1:2] + tail[2:3])
    top = logs[0]
    for one in logs[1:]:
        top = jnp.maximum(top, one)
    shares = [jnp.exp(one - top) for one in logs]
    total = shares[0]
    for one in shares[1:]:
        total = total + one
    inverse = 1.0 / total
    result = None
    for block, share in zip(blocks, shares):
        term = block[:HEAD].astype(jnp.float32) * (share * inverse)
        result = term if result is None else result + term
    return result, top + jnp.log(total)


def layer_kernel(
    tokens, gain, w_query, q_gain, keys_h, values_h, output_h, post_gain, routes, gates,
    w_gate, w_up, w_down, out,
    scaled, weights, partial, arrived, queries, keys, values, values_t, output_weight, scores,
    average_s, average_x, merged_s, merged_z, attended, part, part_r, ordered, held_stream,
    places, mixing, gate_v, up_v, down_v, outgoing, stage, rows_all, normed, product, parts,
    back, returned, final_s, final_r,
    load, ts, tr, ws, wr, ps, pr, qs, qr, fqs, fqr,
    xas, xar, zas, zar, ms, mr, fms, fmr, hs, hr,
    es, er, fs, fr, gs, gr, bs, br, ys, yr,
):
    expert, z, x = here()
    head = lax.axis_index("head")
    core = lax.axis_index("batch")
    f32, bf16 = jnp.float32, jnp.bfloat16
    width = w_query.shape[1] // NX
    rows, features = tokens.shape
    block = queries.shape[2]
    span = rows // NZ
    heads_here = width // HEAD
    sub = span // NH
    count = NZ * sub
    others = [(i, j) for j in range(NB) for i in range(NH) if (i, j) != (0, 0)]

    def columns(owner):
        return pl.ds(pl.multiple_of(owner * width, width), width)

    own_weights = pltpu.make_async_copy(w_query.at[:, columns(x)], weights.at[x], load.at[0])
    own_weights.start()
    load_keys = pltpu.make_async_copy(keys_h, keys, load.at[1])
    load_values = pltpu.make_async_copy(values_h, values, load.at[2])
    load_output = pltpu.make_async_copy(output_h, output_weight, load.at[3])
    load_gate = pltpu.make_async_copy(w_gate, gate_v, load.at[4])
    load_up = pltpu.make_async_copy(w_up, up_v, load.at[5])
    load_down = pltpu.make_async_copy(w_down, down_v, load.at[6])

    @pl.loop(1, NE)
    def _(k):
        signal(expert=lax.rem(expert + k, NE))

    for i, j in others:
        signal(head=lax.rem(head + i, NH), batch=lax.rem(core + j, NB))
    scaled[x] = (tokens[...].astype(f32) * gain[...].astype(f32)).astype(bf16)
    pl.semaphore_wait(pltpu.get_barrier_semaphore(), NE - 1 + len(others))

    def weight_copy(owner, source):
        return remote(
            w_query.at[:, columns(owner)], weights.at[source], ws, wr, expert=z * NX + owner
        )

    def token_copy(target, source):
        return remote(scaled.at[source], scaled.at[source], ts, tr, expert=z * NX + target)

    def sum_copy(target, source):
        return remote(
            partial.at[target], arrived.at[source], ps, pr, expert=target * NX + x
        )

    def all_of(ref, send_sem, recv_sem):
        return remote(ref, ref, send_sem, recv_sem, expert=expert)

    for k in NEAR_FIRST_X:
        target = lax.rem(x + k, NX)
        token_copy(target, x).start()
        weight_copy(target, x).start()
    load_keys.start()
    load_values.start()
    load_output.start()
    slots = 2 * count // 8
    experts = NE * NB
    chosen, weighted = slot_matrix(routes[...], gates[...], experts, 8)
    places[...] = chosen.reshape(experts * slots, count).astype(bf16)
    flat = weighted.reshape(experts * slots, count)
    high = flat.astype(bf16)
    mixing[...] = jnp.concatenate([high, (flat - high.astype(f32)).astype(bf16)], axis=1)
    own_weights.wait()
    all_of(scaled.at[pl.ds(0, NX - 1)], ts, tr).wait_recv()
    all_of(weights.at[pl.ds(0, NX - 1)], ws, wr).wait_recv()
    left = jnp.concatenate([scaled[i] for i in range(NX)], axis=1)
    right = weights[...].reshape(NX * features, width)
    partial[...] = jnp.dot(left, right, preferred_element_type=f32).reshape(NZ, span, width)
    for k in NEAR_FIRST_Z:
        sum_copy(lax.rem(z + k, NZ), z).start()
    arrived[z] = partial[z]
    load_gate.start()
    load_up.start()
    load_down.start()
    load_values.wait()
    for i in range(0, values.shape[0], 128):
        values_t[:, i : i + 128] = values[i : i + 128, :].astype(f32).T.astype(bf16)
    all_of(scaled.at[pl.ds(0, NX - 1)], ts, tr).wait_send()
    all_of(weights.at[pl.ds(0, NX - 1)], ws, wr).wait_send()
    load_keys.wait()
    load_output.wait()
    all_of(arrived.at[pl.ds(0, NZ - 1)], ps, pr).wait_recv()
    total = arrived[0]
    for i in range(1, NZ):
        total = total + arrived[i]
    factor = q_gain[...].astype(f32) / jnp.sqrt(f32(HEAD))
    heads = []
    for h in range(heads_here):
        one = total[:, h * HEAD : (h + 1) * HEAD]
        mean = jnp.mean(one * one, axis=-1, keepdims=True)
        heads.append(one * lax.rsqrt(mean + EPSILON) * factor)
    queries[x, z] = jnp.concatenate(heads, axis=0).astype(bf16)

    def at_step(n):
        near = (n + 1) // 2
        return lax.rem(z + jnp.where(n % 2 == 1, near, NZ - near), NZ)

    def spread(blocks, send_sem, recv_sem):
        for k in NEAR_FIRST_Z:
            remote(
                blocks.at[x, z], blocks.at[x, z], send_sem, recv_sem.at[z],
                expert=lax.rem(z + k, NZ) * NX + x,
            ).start()

    def pass_on(blocks, z_sems, send_sem, recv_sem, n):
        r = at_step(n)
        block = blocks.at[x, r]

        @pl.when(n >= 1)
        def _():
            all_of(block, z_sems[0], z_sems[1].at[r]).wait_recv()

        for k in NEAR_FIRST_X:
            remote(
                block, block, send_sem, recv_sem.at[r], expert=z * NX + lax.rem(x + k, NX)
            ).start()

    def passed(blocks, send_sem, recv_sem, n):
        r = at_step(n)
        return all_of(blocks.at[pl.ds(0, NX - 1), r], send_sem, recv_sem.at[r])

    def attend(n):
        r = at_step(n)
        here_rows = queries[:, r].reshape(NX * block, HEAD)
        average, log_total = transposed_softmax(here_rows, keys, values_t, scores)
        both = with_log(average, log_total)
        for i in range(NX):
            average_s[r, i] = both[:, i * block : (i + 1) * block]
        for k in NEAR_FIRST_X:
            target = lax.rem(x + k, NX)
            remote(
                average_s.at[r, target], average_x.at[r, x], xas, xar.at[r],
                expert=z * NX + target,
            ).start()
        average_x[r, x] = average_s[r, x]

    def merge_x(n):
        r = at_step(n)
        all_of(average_x.at[r, pl.ds(0, NX - 1)], xas, xar.at[r]).wait_recv()
        average, log_total = merged([average_x[r, i] for i in range(NX)])
        merged_s[r] = with_log(average, log_total)

        @pl.when(n == 0)
        def _():
            merged_z[z] = merged_s[z]

        @pl.when(n >= 1)
        def _():
            remote(merged_s.at[r], merged_z.at[z], zas, zar, expert=r * NX + x).start()

    parts_of_z = 2
    per_part = NZ // parts_of_z

    def project(which):
        tall = []
        for n in range(which * per_part, (which + 1) * per_part):
            passed(attended, fms, fmr, n).wait_recv()
            r = at_step(n)
            tall.append(
                jnp.concatenate(
                    [
                        attended[i, r, j * span : (j + 1) * span, :]
                        for i in range(NX)
                        for j in range(heads_here)
                    ],
                    axis=1,
                )
            )
        left = jnp.concatenate(tall, axis=0)
        made = jnp.dot(left, output_weight[...], preferred_element_type=f32)
        made = made.reshape(per_part, NH, sub, features)
        for i in range(NH):
            part[which, i] = made[:, i].reshape(per_part * sub, features)
        for k in (1, 3, 2):
            target = lax.rem(head + k, NH)
            remote(
                part.at[which, target], part_r.at[which, head], hs, hr.at[which], head=target
            ).start()
        part_r[which, head] = part[which, head]

    groups = er.shape[0]
    per_group = NE // groups
    own_group = expert // per_group
    me_hb = head * NB + core
    most = len(others)

    def group_of(step):
        return lax.rem(own_group + step, groups)

    def members(g):
        return pl.ds(g * per_group, per_group)

    def half(owner):
        return pl.ds(pl.multiple_of(owner * slots, slots), slots)

    def target_of(i, j):
        return lax.rem(head + i, NH), lax.rem(core + j, NB)

    def dispatch():
        for which in range(parts_of_z):
            all_of(part_r.at[which, pl.ds(0, NH - 1)], hs, hr.at[which]).wait_recv()
            summed = part_r[which, 0]
            for i in range(1, NH):
                summed = summed + part_r[which, i]
            summed = summed.reshape(per_part, sub, features)
            for n in range(per_part):
                ordered[at_step(which * per_part + n)] = summed[n]
        resid = tokens[...].astype(f32).reshape(NZ, NH, sub, features)
        mine = jnp.zeros((NZ, sub, features), f32)
        for i in range(NH):
            mine = jnp.where(head == i, resid[:, i], mine)
        held_stream[...] = (mine + ordered[...]).reshape(count, features).astype(bf16)
        picked = jnp.dot(places[...], held_stream[...], preferred_element_type=f32)
        outgoing[...] = picked.astype(bf16).reshape(NE, NB * slots, features)

        @pl.loop(1, NE)
        def _(k):
            target = lax.rem(expert + k, NE)
            remote(
                outgoing.at[target], stage.at[expert], es, er.at[own_group], expert=target
            ).start()

        stage[expert] = outgoing[expert]

    def forward():
        @pl.loop(0, groups)
        def _(step):
            g = group_of(step)

            @pl.when(step == 0)
            def _():
                few = stage.at[pl.ds(0, per_group - 1)]
                all_of(few, es, er.at[g]).wait_recv()

            @pl.when(step != 0)
            def _():
                all_of(stage.at[members(g)], es, er.at[g]).wait_recv()

            for i, j in others:
                to_head, to_core = target_of(i, j)
                remote(
                    stage.at[members(g), half(to_core)],
                    rows_all.at[me_hb, members(g)],
                    fs,
                    fr.at[g],
                    head=to_head,
                    batch=to_core,
                ).start()
            rows_all[me_hb, members(g)] = stage[members(g), half(core)]

    ahead = 2
    spread(queries, qs, qr)
    for n in range(ahead):
        pass_on(queries, (qs, qr), fqs, fqr, n)

    @pl.loop(0, NZ)
    def _(n):
        @pl.when(n + ahead < NZ)
        def _():
            pass_on(queries, (qs, qr), fqs, fqr, n + ahead)

        passed(queries, fqs, fqr, n).wait_recv()
        attend(n)

        @pl.when(n >= 1)
        def _():
            merge_x(n - 1)

    merge_x(NZ - 1)
    all_of(queries.at[0, pl.ds(0, NZ - 1)], qs, qr.at[0]).wait_send()
    all_of(queries.at[pl.ds(0, NX - 1)], fqs, fqr.at[0]).wait_send()
    all_of(average_s.at[:, pl.ds(0, NX - 1)], xas, xar.at[0]).wait_send()
    all_of(arrived.at[pl.ds(0, NZ - 1)], ps, pr).wait_send()
    all_of(merged_z.at[pl.ds(0, NZ - 1)], zas, zar).wait_recv()
    average, _ = merged([merged_z[i] for i in range(NZ)])
    attended[x, z] = average.T.astype(bf16)
    spread(attended, ms, mr)
    for n in range(NZ):
        pass_on(attended, (ms, mr), fms, fmr, n)
    for which in range(parts_of_z):
        project(which)
    dispatch()
    load_gate.wait()
    load_up.wait()
    load_down.wait()
    all_of(merged_s.at[pl.ds(0, NZ - 1)], zas, zar).wait_send()
    all_of(attended.at[0, pl.ds(0, NZ - 1)], ms, mr.at[0]).wait_send()
    all_of(attended.at[pl.ds(0, NX - 1)], fms, fmr.at[0]).wait_send()
    all_of(part.at[:, pl.ds(0, NH - 1)], hs, hr.at[0]).wait_send()
    forward()
    all_of(outgoing.at[pl.ds(0, NE - 1)], es, er.at[0]).wait_send()

    held = NH * NB * slots
    square = jnp.zeros((held, features), f32)
    for g in range(groups):
        for e in range(g * per_group, (g + 1) * per_group):
            if e == g * per_group:
                all_of(rows_all.at[pl.ds(0, most), members(g)], fs, fr.at[g]).wait_recv()
            wide = rows_all[:, e].reshape(held, features).astype(f32)
            square = square + wide * wide
    mean = jnp.sum(square, axis=1, keepdims=True) * (1.0 / (NE * features))
    scale = lax.rsqrt(mean + EPSILON)
    for e in range(NE):
        wide = rows_all[:, e].reshape(held, features).astype(f32)
        normed[:, e * features : (e + 1) * features] = (
            wide * scale * post_gain[e : e + 1, :].astype(f32)
        ).astype(bf16)
    gate_part = jnp.dot(normed[...], gate_v[...], preferred_element_type=f32)
    up_part = jnp.dot(normed[...], up_v[...], preferred_element_type=f32)
    hidden = (gate_part / (1.0 + jnp.exp(-gate_part)) * up_part).astype(bf16)
    reach = parts.shape[-1]
    bands = parts.shape[0]
    per_band = NE // bands

    for g in range(bands):
        made = jnp.dot(hidden, down_v[:, g * reach : (g + 1) * reach], preferred_element_type=f32)
        product[g] = made.astype(bf16).reshape(NH * NB, slots, reach)
        for i, j in others:
            to_head, to_core = target_of(i, j)
            remote(
                product.at[g, to_head * NB + to_core],
                parts.at[g, me_hb],
                gs,
                gr.at[g],
                head=to_head,
                batch=to_core,
            ).start()
        parts[g, me_hb] = product[g, me_hb]

    for g in range(bands):
        all_of(parts.at[g, pl.ds(0, most)], gs, gr.at[g]).wait_recv()
        total = parts[g, 0:NB].astype(f32)
        for i in range(1, NH):
            total = total + parts[g, i * NB : (i + 1) * NB].astype(f32)
        total = total.reshape(NB * slots, reach).astype(bf16)
        for k in range(per_band):
            back[g * per_band + k] = total[:, k * features : (k + 1) * features]

        @pl.loop(0, per_band)
        def _(k):
            target = g * per_band + k

            @pl.when(target != expert)
            def _():
                remote(back.at[target], returned.at[expert], bs, br, expert=target).start()

    returned[expert] = back[expert]
    all_of(rows_all.at[pl.ds(0, most)], fs, fr.at[0]).wait_send()
    all_of(product.at[:, pl.ds(0, most)], gs, gr.at[0]).wait_send()
    all_of(returned.at[pl.ds(0, NE - 1)], bs, br).wait_recv()
    both = lax.dot_general(
        mixing[...],
        returned[...].reshape(experts * slots, features),
        (((0,), (0,)), ((), ())),
        preferred_element_type=f32,
    )
    mixture = both[:count] + both[count:]
    final_s[...] = (held_stream[...].astype(f32) + mixture).astype(bf16)
    for k in (1, 3, 2):
        remote(final_s, final_r.at[head], ys, yr, head=lax.rem(head + k, NH)).start()
    final_r[head] = final_s[...]
    all_of(back.at[pl.ds(0, NE - 1)], bs, br).wait_send()
    all_of(final_r.at[pl.ds(0, NH - 1)], ys, yr).wait_recv()
    pieces = [final_r[i].astype(f32).reshape(NZ, sub, features) for i in range(NH)]
    out[...] = jnp.concatenate(
        [pieces[i][r] for r in range(NZ) for i in range(NH)], axis=0
    ).astype(bf16)
    all_of(final_r.at[pl.ds(0, NH - 1)], ys, yr).wait_send()


def on_device(
    tokens, attn_gain, w_query, q_gain, cached_keys, prefix_values, output_weight,
    post_gain, routes, route_gates, w_gate, w_up, w_down,
):
    rows, features = tokens.shape
    width = w_query.shape[1] // NX
    block = rows * w_query.shape[1] // HEAD // NE
    bf16, f32 = jnp.bfloat16, jnp.float32
    keys = cached_keys.shape[0]
    span = rows // NZ
    sub = span // NH
    count = NZ * sub
    halves = 2
    head = lax.axis_index("head")
    top = routes.shape[1]

    def mine(table):
        cut = lax.dynamic_index_in_dim(table.reshape(NZ, NH, sub, top), head, 1, False)
        return cut.reshape(count, top).T

    model, ff = w_gate.shape[1:]
    slots = 2 * count // 8
    groups = 2
    bands = 4
    experts = NE * NB
    V = pltpu.VMEM
    return pl.pallas_call(
        layer_kernel,
        out_shape=jax.ShapeDtypeStruct((rows, features), bf16),
        in_specs=[IN_VMEM, IN_VMEM, IN_ANY, IN_VMEM] + [IN_ANY] * 3 + [IN_VMEM] * 3 + [IN_ANY] * 3,
        out_specs=IN_VMEM,
        scratch_shapes=[
            V((NX, rows, features), bf16),
            V((NX, features, width), bf16),
            V((NZ, span, width), f32),
            V((NZ, span, width), f32),
            V((NX, NZ, block, HEAD), bf16),
            V((keys, HEAD), bf16),
            V((keys, HEAD), bf16),
            V((HEAD, keys), bf16),
            V(output_weight.shape, bf16),
            V((keys, NX * block), f32),
            V((NZ, NX, HEAD + LOG_ROWS, block), bf16),
            V((NZ, NX, HEAD + LOG_ROWS, block), bf16),
            V((NZ, HEAD + LOG_ROWS, block), bf16),
            V((NZ, HEAD + LOG_ROWS, block), bf16),
            V((NX, NZ, block, HEAD), bf16),
            V((halves, NH, count // halves, features), f32),
            V((halves, NH, count // halves, features), f32),
            V((NZ, sub, features), f32),
            V((count, features), bf16),
            V((experts * slots, count), bf16),
            V((experts * slots, 2 * count), bf16),
            V((model, ff), bf16),
            V((model, ff), bf16),
            V((ff, model), bf16),
            V((NE, NB * slots, features), bf16),
            V((NE, NB * slots, features), bf16),
            V((NH * NB, NE, slots, features), bf16),
            V((NH * NB * slots, model), bf16),
            V((bands, NH * NB, slots, model // bands), bf16),
            V((bands, NH * NB, slots, model // bands), bf16),
            V((NE, NB * slots, features), bf16),
            V((NE, NB * slots, features), bf16),
            V((count, features), bf16),
            V((NH, count, features), bf16),
            DMA((7,)),
            DMA, DMA, DMA, DMA,
            DMA, DMA,
            DMA, DMA((NZ,)), DMA, DMA((NZ,)),
            DMA, DMA((NZ,)), DMA, DMA,
            DMA, DMA((NZ,)), DMA, DMA((NZ,)),
            DMA, DMA((halves,)),
            DMA, DMA((groups,)), DMA, DMA((groups,)),
            DMA, DMA((bands,)), DMA, DMA, DMA, DMA,
        ],
        compiler_params=pltpu.CompilerParams(
            collective_id=1, has_side_effects=True, vmem_limit_bytes=56 * MIB
        ),
        name="scoring_layer",
    )(
        tokens, attn_gain[None, :], w_query, q_gain[None, :],
        cached_keys, prefix_values, output_weight,
        post_gain.reshape(NE, features), mine(routes), mine(route_gates),
        w_gate[0], w_up[0], w_down[0],
    )


def solution(mesh):
    placed = (
        P("batch", "expert"),
        P("expert"),
        P("expert", "head"),
        P(),
        P("expert", "head"),
        P("expert", "head"),
        P("head", "expert"),
        P(),
        P("batch", None),
        P("batch", None),
        P(("expert", "batch"), None, "head"),
        P(("expert", "batch"), None, "head"),
        P(("expert", "batch"), "head", None),
    )
    return jax.shard_map(
        on_device, mesh=mesh, in_specs=placed, out_specs=P("batch", "expert"), check_vma=False
    )
```

time: 161 us -> 143 us (0.89)
  the two profiles are of different devices: /device:TPU:224 before, /device:TPU:192 now
where the time goes in v3:
time: 143 us
  Pallas kernels  138 us (97%)
  local copies, waits for them, and re-layouts  4.66 us (3%)
    pallas_call x1, Pallas kernels, on_device(): pl.pallas_call(layer_kernel, out_shape=jax.ShapeDtypeStruct((rows, featur...  138 us

profile of v3, /device:TPU:192, one launch (start us, length us, event | category | flops | bytes accessed | tf_op | source)
XLA Modules:
  0.0 143.1 jit_solution(17807213148298392329)
XLA Ops:
  0.0 0.9 reshape.18
  0.9 0.7 reshape.19
  1.6 0.9 reshape.20
  2.6 0.7 reshape.21
  3.2 138.4 %scoring_layer.1 = bf16[256,128]{1,0:T(8,128)(2,1)} custom-call(bf16[256,128]{1,0:T(8,128)(2,1)} %tokens.1, bf16[1,128]{1,0:T(2,128)(2,1)} %bitcast.30, bf16[128,2048]{1,0:T(8,128)(2,1)} %w_query.1, bf16[1,128]{1,0:T(2,128)(2,1)} %bitcast.31, bf16[4096,128]{1,0:T(8,128)(2,1)} %keys_h.1, bf16[4096,128]{1,0:T(8,128)(2,1)} %values_h.1, ...), custom_call_target="tpu_custom_call" | custom-call | tf_op jit(solution)/shard_map/scoring_layer/pallas_call | solution.py:540
  141.7 1.5 %copy.19 = bf16[256,128]{1,0:T(8,128)(2,1)} copy(bf16[256,128]{1,0:T(8,128)(2,1)} %scoring_layer.1) | data formatting | bytes 131072
  (2 shorter events, 0.1 us)

commit v4 on v3

--- a/solution.py
+++ b/solution.py
@@ -20,6 +20,7 @@
 DMA = pltpu.SemaphoreType.DMA
 NEAR_FIRST_Z = (1, 7, 2, 6, 3, 5, 4)
 NEAR_FIRST_X = (1, 3, 2)
+ATTEND_ORDER = (0, 1, 6, 4, 3, 5, 2, 7)
 
 
 def remote(src, dst, send_sem, recv_sem, **where):
@@ -196,13 +197,6 @@
     load_keys.start()
     load_values.start()
     load_output.start()
-    slots = 2 * count // 8
-    experts = NE * NB
-    chosen, weighted = slot_matrix(routes[...], gates[...], experts, 8)
-    places[...] = chosen.reshape(experts * slots, count).astype(bf16)
-    flat = weighted.reshape(experts * slots, count)
-    high = flat.astype(bf16)
-    mixing[...] = jnp.concatenate([high, (flat - high.astype(f32)).astype(bf16)], axis=1)
     own_weights.wait()
     all_of(scaled.at[pl.ds(0, NX - 1)], ts, tr).wait_recv()
     all_of(weights.at[pl.ds(0, NX - 1)], ws, wr).wait_recv()
@@ -215,6 +209,23 @@
     load_gate.start()
     load_up.start()
     load_down.start()
+    slots = 2 * count // 8
+    experts = NE * NB
+    token = lax.broadcasted_iota(jnp.int32, (rows, count), 0)
+    owned = lax.broadcasted_iota(jnp.int32, (rows, count), 1)
+    mine = (token == owned // sub * span + head * sub + owned % sub).astype(f32)
+
+    def own(table):
+        return jnp.dot(
+            table, mine, precision=lax.Precision.HIGHEST, preferred_element_type=f32
+        )
+
+    own_routes = own(routes[...].astype(f32)).astype(jnp.int32)
+    chosen, weighted = slot_matrix(own_routes, own(gates[...]), experts, 8)
+    places[...] = chosen.reshape(experts * slots, count).astype(bf16)
+    flat = weighted.reshape(experts * slots, count)
+    high = flat.astype(bf16)
+    mixing[...] = jnp.concatenate([high, (flat - high.astype(f32)).astype(bf16)], axis=1)
     load_values.wait()
     for i in range(0, values.shape[0], 128):
         values_t[:, i : i + 128] = values[i : i + 128, :].astype(f32).T.astype(bf16)
@@ -238,6 +249,12 @@
         near = (n + 1) // 2
         return lax.rem(z + jnp.where(n % 2 == 1, near, NZ - near), NZ)
 
+    def at_turn(n):
+        offset = ATTEND_ORDER[NZ - 1]
+        for i in range(NZ - 1):
+            offset = jnp.where(n == i, ATTEND_ORDER[i], offset)
+        return lax.rem(z + offset, NZ)
+
     def spread(blocks, send_sem, recv_sem):
         for k in NEAR_FIRST_Z:
             remote(
@@ -245,8 +262,8 @@
                 expert=lax.rem(z + k, NZ) * NX + x,
             ).start()
 
-    def pass_on(blocks, z_sems, send_sem, recv_sem, n):
-        r = at_step(n)
+    def pass_on(blocks, z_sems, send_sem, recv_sem, n, order):
+        r = order(n)
         block = blocks.at[x, r]
 
         @pl.when(n >= 1)
@@ -258,12 +275,12 @@
                 block, block, send_sem, recv_sem.at[r], expert=z * NX + lax.rem(x + k, NX)
             ).start()
 
-    def passed(blocks, send_sem, recv_sem, n):
-        r = at_step(n)
+    def passed(blocks, send_sem, recv_sem, n, order):
+        r = order(n)
         return all_of(blocks.at[pl.ds(0, NX - 1), r], send_sem, recv_sem.at[r])
 
     def attend(n):
-        r = at_step(n)
+        r = at_turn(n)
         here_rows = queries[:, r].reshape(NX * block, HEAD)
         average, log_total = transposed_softmax(here_rows, keys, values_t, scores)
         both = with_log(average, log_total)
@@ -278,7 +295,7 @@
         average_x[r, x] = average_s[r, x]
 
     def merge_x(n):
-        r = at_step(n)
+        r = at_turn(n)
         all_of(average_x.at[r, pl.ds(0, NX - 1)], xas, xar.at[r]).wait_recv()
         average, log_total = merged([average_x[r, i] for i in range(NX)])
         merged_s[r] = with_log(average, log_total)
@@ -297,7 +314,7 @@
     def project(which):
         tall = []
         for n in range(which * per_part, (which + 1) * per_part):
-            passed(attended, fms, fmr, n).wait_recv()
+            passed(attended, fms, fmr, n, at_step).wait_recv()
             r = at_step(n)
             tall.append(
                 jnp.concatenate(
@@ -356,8 +373,10 @@
         picked = jnp.dot(places[...], held_stream[...], preferred_element_type=f32)
         outgoing[...] = picked.astype(bf16).reshape(NE, NB * slots, features)
 
-        @pl.loop(1, NE)
-        def _(k):
+        @pl.loop(0, NE - 1)
+        def _(n):
+            step = (n + 1) // 2
+            k = NE // 2 + jnp.where(n % 2 == 1, step, -step)
             target = lax.rem(expert + k, NE)
             remote(
                 outgoing.at[target], stage.at[expert], es, er.at[own_group], expert=target
@@ -394,21 +413,22 @@
     ahead = 2
     spread(queries, qs, qr)
     for n in range(ahead):
-        pass_on(queries, (qs, qr), fqs, fqr, n)
+        pass_on(queries, (qs, qr), fqs, fqr, n, at_turn)
 
     @pl.loop(0, NZ)
     def _(n):
         @pl.when(n + ahead < NZ)
         def _():
-            pass_on(queries, (qs, qr), fqs, fqr, n + ahead)
-
-        passed(queries, fqs, fqr, n).wait_recv()
+            pass_on(queries, (qs, qr), fqs, fqr, n + ahead, at_turn)
+
+        passed(queries, fqs, fqr, n, at_turn).wait_recv()
         attend(n)
 
-        @pl.when(n >= 1)
+        @pl.when(n >= 2)
         def _():
-            merge_x(n - 1)
-
+            merge_x(n - 2)
+
+    merge_x(NZ - 2)
     merge_x(NZ - 1)
     all_of(queries.at[0, pl.ds(0, NZ - 1)], qs, qr.at[0]).wait_send()
     all_of(queries.at[pl.ds(0, NX - 1)], fqs, fqr.at[0]).wait_send()
@@ -419,7 +439,7 @@
     attended[x, z] = average.T.astype(bf16)
     spread(attended, ms, mr)
     for n in range(NZ):
-        pass_on(attended, (ms, mr), fms, fmr, n)
+        pass_on(attended, (ms, mr), fms, fmr, n, at_step)
     for which in range(parts_of_z):
         project(which)
     dispatch()
@@ -455,8 +475,11 @@
     bands = parts.shape[0]
     per_band = NE // bands
 
-    for g in range(bands):
-        made = jnp.dot(hidden, down_v[:, g * reach : (g + 1) * reach], preferred_element_type=f32)
+    own_band = expert // per_band
+    band_order = [lax.rem(own_band + i, bands) for i in (2, 1, 3, 0)]
+    for g in band_order:
+        lanes = pl.ds(pl.multiple_of(g * reach, reach), reach)
+        made = jnp.dot(hidden, down_v[:, lanes], preferred_element_type=f32)
         product[g] = made.astype(bf16).reshape(NH * NB, slots, reach)
         for i, j in others:
             to_head, to_core = target_of(i, j)
@@ -470,11 +493,11 @@
             ).start()
         parts[g, me_hb] = product[g, me_hb]
 
-    for g in range(bands):
+    for g in band_order:
         all_of(parts.at[g, pl.ds(0, most)], gs, gr.at[g]).wait_recv()
-        total = parts[g, 0:NB].astype(f32)
+        total = parts[g, pl.ds(0, NB)].astype(f32)
         for i in range(1, NH):
-            total = total + parts[g, i * NB : (i + 1) * NB].astype(f32)
+            total = total + parts[g, pl.ds(i * NB, NB)].astype(f32)
         total = total.reshape(NB * slots, reach).astype(bf16)
         for k in range(per_band):
             back[g * per_band + k] = total[:, k * features : (k + 1) * features]
@@ -524,12 +547,6 @@
     sub = span // NH
     count = NZ * sub
     halves = 2
-    head = lax.axis_index("head")
-    top = routes.shape[1]
-
-    def mine(table):
-        cut = lax.dynamic_index_in_dim(table.reshape(NZ, NH, sub, top), head, 1, False)
-        return cut.reshape(count, top).T
 
     model, ff = w_gate.shape[1:]
     slots = 2 * count // 8
@@ -594,7 +611,7 @@
     )(
         tokens, attn_gain[None, :], w_query, q_gain[None, :],
         cached_keys, prefix_values, output_weight,
-        post_gain.reshape(NE, features), mine(routes), mine(route_gates),
+        post_gain.reshape(NE, features), routes.T, route_gates.T,
         w_gate[0], w_up[0], w_down[0],
     )
 

time: 143 us -> 134 us (0.937)
  the two profiles are of different devices: /device:TPU:192 before, /device:TPU:2 now
where the time goes in v4:
time: 134 us
  Pallas kernels  133 us (99%)
  local copies, waits for them, and re-layouts  1.47 us (1%)
    pallas_call x1, Pallas kernels, on_device(): pl.pallas_call(layer_kernel, out_shape=jax.ShapeDtypeStruct((rows, featur...  133 us

profile of v4, /device:TPU:2, one launch (start us, length us, event | category | flops | bytes accessed | tf_op | source)
XLA Modules:
  0.0 134.1 jit_solution(12980627968267679901)
XLA Ops:
  0.0 132.6 %scoring_layer.1 = bf16[256,128]{1,0:T(8,128)(2,1)} custom-call(bf16[256,128]{1,0:T(8,128)(2,1)} %tokens.1, bf16[1,128]{1,0:T(2,128)(2,1)} %bitcast.14, bf16[128,2048]{1,0:T(8,128)(2,1)} %w_query.1, bf16[1,128]{1,0:T(2,128)(2,1)} %bitcast.15, bf16[4096,128]{1,0:T(8,128)(2,1)} %keys_h.1, bf16[4096,128]{1,0:T(8,128)(2,1)} %values_h.1, ...), custom_call_target="tpu_custom_call" | custom-call | tf_op jit(solution)/shard_map/scoring_layer/pallas_call | solution.py:557
  132.6 1.5 %copy.15 = bf16[256,128]{1,0:T(8,128)(2,1)} copy(bf16[256,128]{1,0:T(8,128)(2,1)} %scoring_layer.1) | data formatting | bytes 131072

commit v5 on v4

--- a/solution.py
+++ b/solution.py
@@ -20,6 +20,7 @@
 DMA = pltpu.SemaphoreType.DMA
 NEAR_FIRST_Z = (1, 7, 2, 6, 3, 5, 4)
 NEAR_FIRST_X = (1, 3, 2)
+FAR_FIRST_Z = (4, 3, 5, 2, 6, 1, 7)
 ATTEND_ORDER = (0, 1, 6, 4, 3, 5, 2, 7)
 
 
@@ -203,7 +204,7 @@
     left = jnp.concatenate([scaled[i] for i in range(NX)], axis=1)
     right = weights[...].reshape(NX * features, width)
     partial[...] = jnp.dot(left, right, preferred_element_type=f32).reshape(NZ, span, width)
-    for k in NEAR_FIRST_Z:
+    for k in FAR_FIRST_Z:
         sum_copy(lax.rem(z + k, NZ), z).start()
     arrived[z] = partial[z]
     load_gate.start()
@@ -225,7 +226,8 @@
     places[...] = chosen.reshape(experts * slots, count).astype(bf16)
     flat = weighted.reshape(experts * slots, count)
     high = flat.astype(bf16)
-    mixing[...] = jnp.concatenate([high, (flat - high.astype(f32)).astype(bf16)], axis=1)
+    low = flat - high.astype(f32)
+    mixing[...] = jnp.concatenate([high.astype(f32), low], axis=1).T.astype(bf16)
     load_values.wait()
     for i in range(0, values.shape[0], 128):
         values_t[:, i : i + 128] = values[i : i + 128, :].astype(f32).T.astype(bf16)
@@ -430,10 +432,6 @@
 
     merge_x(NZ - 2)
     merge_x(NZ - 1)
-    all_of(queries.at[0, pl.ds(0, NZ - 1)], qs, qr.at[0]).wait_send()
-    all_of(queries.at[pl.ds(0, NX - 1)], fqs, fqr.at[0]).wait_send()
-    all_of(average_s.at[:, pl.ds(0, NX - 1)], xas, xar.at[0]).wait_send()
-    all_of(arrived.at[pl.ds(0, NZ - 1)], ps, pr).wait_send()
     all_of(merged_z.at[pl.ds(0, NZ - 1)], zas, zar).wait_recv()
     average, _ = merged([merged_z[i] for i in range(NZ)])
     attended[x, z] = average.T.astype(bf16)
@@ -446,6 +444,10 @@
     load_gate.wait()
     load_up.wait()
     load_down.wait()
+    all_of(queries.at[0, pl.ds(0, NZ - 1)], qs, qr.at[0]).wait_send()
+    all_of(queries.at[pl.ds(0, NX - 1)], fqs, fqr.at[0]).wait_send()
+    all_of(average_s.at[:, pl.ds(0, NX - 1)], xas, xar.at[0]).wait_send()
+    all_of(arrived.at[pl.ds(0, NZ - 1)], ps, pr).wait_send()
     all_of(merged_s.at[pl.ds(0, NZ - 1)], zas, zar).wait_send()
     all_of(attended.at[0, pl.ds(0, NZ - 1)], ms, mr.at[0]).wait_send()
     all_of(attended.at[pl.ds(0, NX - 1)], fms, fmr.at[0]).wait_send()
@@ -514,10 +516,9 @@
     all_of(rows_all.at[pl.ds(0, most)], fs, fr.at[0]).wait_send()
     all_of(product.at[:, pl.ds(0, most)], gs, gr.at[0]).wait_send()
     all_of(returned.at[pl.ds(0, NE - 1)], bs, br).wait_recv()
-    both = lax.dot_general(
+    both = jnp.dot(
         mixing[...],
         returned[...].reshape(experts * slots, features),
-        (((0,), (0,)), ((), ())),
         preferred_element_type=f32,
     )
     mixture = both[:count] + both[count:]
@@ -580,7 +581,7 @@
             V((NZ, sub, features), f32),
             V((count, features), bf16),
             V((experts * slots, count), bf16),
-            V((experts * slots, 2 * count), bf16),
+            V((2 * count, experts * slots), bf16),
             V((model, ff), bf16),
             V((model, ff), bf16),
             V((ff, model), bf16),

time: 134 us -> 134 us (level)
  no operation moved by 1% of the time
where the time goes in v5:
time: 134 us
  Pallas kernels  132 us (99%)
  local copies, waits for them, and re-layouts  1.47 us (1%)
    pallas_call x1, Pallas kernels, on_device(): pl.pallas_call(layer_kernel, out_shape=jax.ShapeDtypeStruct((rows, featur...  132 us

profile of v5, /device:TPU:2, one launch (start us, length us, event | category | flops | bytes accessed | tf_op | source)
XLA Modules:
  0.0 133.5 jit_solution(4546926151914580223)
XLA Ops:
  0.0 132.0 %scoring_layer.1 = bf16[256,128]{1,0:T(8,128)(2,1)} custom-call(bf16[256,128]{1,0:T(8,128)(2,1)} %tokens.1, bf16[1,128]{1,0:T(2,128)(2,1)} %bitcast.14, bf16[128,2048]{1,0:T(8,128)(2,1)} %w_query.1, bf16[1,128]{1,0:T(2,128)(2,1)} %bitcast.15, bf16[4096,128]{1,0:T(8,128)(2,1)} %keys_h.1, bf16[4096,128]{1,0:T(8,128)(2,1)} %values_h.1, ...), custom_call_target="tpu_custom_call" | custom-call | tf_op jit(solution)/shard_map/scoring_layer/pallas_call | solution.py:558
  132.1 1.5 %copy.15 = bf16[256,128]{1,0:T(8,128)(2,1)} copy(bf16[256,128]{1,0:T(8,128)(2,1)} %scoring_layer.1) | data formatting | bytes 131072

commit v6 on v5

--- a/solution.py
+++ b/solution.py
@@ -137,7 +137,7 @@
     average_s, average_x, merged_s, merged_z, attended, part, part_r, ordered, held_stream,
     places, mixing, gate_v, up_v, down_v, outgoing, stage, rows_all, normed, product, parts,
     back, returned, final_s, final_r,
-    load, ts, tr, ws, wr, ps, pr, qs, qr, fqs, fqr,
+    load, ts, tr, ws, wr, cs, cr, ps, pr, qs, qr, fqs, fqr,
     xas, xar, zas, zar, ms, mr, fms, fmr, hs, hr,
     es, er, fs, fr, gs, gr, bs, br, ys, yr,
 ):
@@ -175,9 +175,18 @@
     scaled[x] = (tokens[...].astype(f32) * gain[...].astype(f32)).astype(bf16)
     pl.semaphore_wait(pltpu.get_barrier_semaphore(), NE - 1 + len(others))
 
+    half_features = features // NB
+    my_half = pl.ds(pl.multiple_of(core * half_features, half_features), half_features)
+
     def weight_copy(owner, source):
         return remote(
-            w_query.at[:, columns(owner)], weights.at[source], ws, wr, expert=z * NX + owner
+            w_query.at[my_half, columns(owner)], weights.at[source, my_half], ws, wr,
+            expert=z * NX + owner,
+        )
+
+    def core_copy(source):
+        return remote(
+            weights.at[source, my_half], weights.at[source, my_half], cs, cr, batch=1 - core
         )
 
     def token_copy(target, source):
@@ -193,14 +202,19 @@
 
     for k in NEAR_FIRST_X:
         target = lax.rem(x + k, NX)
-        token_copy(target, x).start()
         weight_copy(target, x).start()
+    for k in NEAR_FIRST_X:
+        token_copy(lax.rem(x + k, NX), x).start()
     load_keys.start()
     load_values.start()
     load_output.start()
     own_weights.wait()
+    some = weights.at[pl.ds(0, NX - 1), pl.ds(0, half_features)]
+    all_of(some, ws, wr).wait_recv()
+    for k in NEAR_FIRST_X:
+        core_copy(lax.rem(x + k, NX)).start()
     all_of(scaled.at[pl.ds(0, NX - 1)], ts, tr).wait_recv()
-    all_of(weights.at[pl.ds(0, NX - 1)], ws, wr).wait_recv()
+    all_of(some, cs, cr).wait_recv()
     left = jnp.concatenate([scaled[i] for i in range(NX)], axis=1)
     right = weights[...].reshape(NX * features, width)
     partial[...] = jnp.dot(left, right, preferred_element_type=f32).reshape(NZ, span, width)
@@ -232,7 +246,8 @@
     for i in range(0, values.shape[0], 128):
         values_t[:, i : i + 128] = values[i : i + 128, :].astype(f32).T.astype(bf16)
     all_of(scaled.at[pl.ds(0, NX - 1)], ts, tr).wait_send()
-    all_of(weights.at[pl.ds(0, NX - 1)], ws, wr).wait_send()
+    all_of(some, ws, wr).wait_send()
+    all_of(some, cs, cr).wait_send()
     load_keys.wait()
     load_output.wait()
     all_of(arrived.at[pl.ds(0, NZ - 1)], ps, pr).wait_recv()
@@ -596,7 +611,7 @@
             V((count, features), bf16),
             V((NH, count, features), bf16),
             DMA((7,)),
-            DMA, DMA, DMA, DMA,
+            DMA, DMA, DMA, DMA, DMA, DMA,
             DMA, DMA,
             DMA, DMA((NZ,)), DMA, DMA((NZ,)),
             DMA, DMA((NZ,)), DMA, DMA,

time: 134 us -> 132 us (0.985)
    pallas_call x1, Pallas kernels: 132 us -> 131 us  [on_device(): pl.pallas_call(layer_kernel, out_shape=jax.ShapeDtypeStruct((rows, featur...]
where the time goes in v6:
time: 132 us
  Pallas kernels  131 us (99%)
  local copies, waits for them, and re-layouts  1.47 us (1%)
    pallas_call x1, Pallas kernels, on_device(): pl.pallas_call(layer_kernel, out_shape=jax.ShapeDtypeStruct((rows, featur...  131 us

profile of v6, /device:TPU:2, one launch (start us, length us, event | category | flops | bytes accessed | tf_op | source)
XLA Modules:
  0.0 132.0 jit_solution(11750274347982139934)
XLA Ops:
  0.0 130.5 %scoring_layer.1 = bf16[256,128]{1,0:T(8,128)(2,1)} custom-call(bf16[256,128]{1,0:T(8,128)(2,1)} %tokens.1, bf16[1,128]{1,0:T(2,128)(2,1)} %bitcast.14, bf16[128,2048]{1,0:T(8,128)(2,1)} %w_query.1, bf16[1,128]{1,0:T(2,128)(2,1)} %bitcast.15, bf16[4096,128]{1,0:T(8,128)(2,1)} %keys_h.1, bf16[4096,128]{1,0:T(8,128)(2,1)} %values_h.1, ...), custom_call_target="tpu_custom_call" | custom-call | tf_op jit(solution)/shard_map/scoring_layer/pallas_call | solution.py:573
  130.6 1.5 %copy.15 = bf16[256,128]{1,0:T(8,128)(2,1)} copy(bf16[256,128]{1,0:T(8,128)(2,1)} %scoring_layer.1) | data formatting | bytes 131072
